TPU v7x, 32 devices: a whole 2x2x4 slice. The times are simulated.
32 devices in a mesh: parts: 2 (over y), seq: 8 (over z, x), head: 2 (over core).
Axes of the slice: x: 2, y: 2, z: 4, core: 2. Of those that a mesh axis runs over, the one named last changes fastest.
Arguments:
- query_states: bfloat16 [4096, 8192], P(('parts', 'seq', 'head')), parts along dimension 0, may hold values from -80 to 80, as said below
- key_states: bfloat16 [4096, 1024], P(('parts', 'seq', 'head')), parts along dimension 0, may hold values from -6 to 6
- value_states: bfloat16 [4096, 1024], P(('parts', 'seq', 'head')), parts along dimension 0, may hold values from -12 to 12
- vertical_blocks: int32 [16, 6], P('parts'), parts along dimension 0, may hold values from 0 to 31, as said below
- slash_offsets: int32 [16, 6], P('parts'), parts along dimension 0, may hold values from 0 to 7, as said below
Outputs:
- attended: bfloat16 [4096, 8192], P(('parts', 'seq', 'head')), parts along dimension 0
There are 2 independent parts, one for each index of `parts`. A program takes and returns all parts, laid end to end along the dimension named above; each array names one. Nothing has to cross between parts.
Inputs may be any that keep to these rules, and one draw needn't show every extreme that they name: `query_states`: entries of order one, a few larger. `vertical_blocks`: each row lists 6 different key blocks, among them block 0. `slash_offsets`: each row lists 6 different block offsets, among them 0 and 1.
All inputs are finite; a program needn't handle non-finite values.
Results may differ from a plain program's by a relative error of at most 0.0034.
Values may be sent and summed in bfloat16 or wider, within the bound.
A program may use at most 64 MiB of HBM per device.

v0:
```python
import math

import jax
import jax.numpy as jnp
from jax import lax
from jax.sharding import PartitionSpec as P

BS = 64
SPAN = 8


def passed_along(block, axis, distance):
    devices = range(lax.axis_size(axis))
    route = [(i - distance, i) for i in devices if i - distance in devices]
    return lax.ppermute(block, axis, route)


def block_mask(query_block, slash_here, vertical_here):
    positions = jnp.arange(BS, dtype=jnp.int32)
    causal = positions[None, :] <= positions[:, None]
    key_block = query_block - slash_here
    slash_ok = (key_block >= 0)[:, :, None, None] & (
        (slash_here != 0)[:, :, None, None] | causal[None, None]
    )
    slash_ok = jnp.transpose(slash_ok, (0, 2, 1, 3)).reshape(slash_here.shape[0], BS, -1)
    on_slash = jnp.any((query_block - vertical_here)[:, :, None] == slash_here[:, None, :], axis=-1)
    vertical_ok = (vertical_here <= query_block) & jnp.logical_not(on_slash)
    vertical_ok = jnp.broadcast_to(
        vertical_ok[:, None, :, None], (vertical_here.shape[0], BS, vertical_here.shape[1], BS)
    )
    vertical_ok = vertical_ok.reshape(vertical_here.shape[0], BS, -1)
    return jnp.concatenate([slash_ok, vertical_ok], axis=-1)


def attend_block(query_tile, key_rows, value_rows, active, score_scale):
    scores = (
        jnp.einsum("tgch,gkh->gctk", query_tile, key_rows, preferred_element_type=jnp.float32)
        * score_scale
    )
    scores = jnp.where(active[:, None], scores, -jnp.inf)
    row_max = jnp.max(scores, axis=-1, keepdims=True)
    weights = jnp.exp(scores - row_max)
    row_total = jnp.sum(weights, axis=-1)
    rounded = weights.astype(jnp.bfloat16)
    mixed_rows = jnp.einsum(
        "gctk,gkh->tgch", rounded, value_rows, preferred_element_type=jnp.float32
    )
    mixed_rows = mixed_rows / jnp.transpose(row_total, (2, 0, 1))[..., None]
    return mixed_rows.astype(jnp.bfloat16)


def owned_columns(key_here, value_here, vertical_here, first_block):
    block_count = key_here.shape[0] // BS
    kv_heads = vertical_here.shape[0]
    head_dim = key_here.shape[1] // kv_heads
    key_blocks = key_here.reshape(block_count, BS, kv_heads, head_dim)
    value_blocks = value_here.reshape(block_count, BS, kv_heads, head_dim)
    offset = vertical_here - first_block
    inside = ((offset >= 0) & (offset < block_count))[:, :, None, None]
    picked = jnp.clip(offset, 0, block_count - 1)
    head_rows = jnp.arange(kv_heads, dtype=jnp.int32)[:, None]
    zero_fill = jnp.zeros((), jnp.float32)
    key_cols = jnp.where(inside, key_blocks[picked, :, head_rows, :].astype(jnp.float32), zero_fill)
    value_cols = jnp.where(
        inside, value_blocks[picked, :, head_rows, :].astype(jnp.float32), zero_fill
    )
    return (key_cols, value_cols)


def attend_rows(
    query_here,
    key_ext,
    value_ext,
    ext_first,
    query_first,
    column_keys,
    column_values,
    vertical_here,
    slash_here,
):
    length = query_here.shape[0]
    kv_heads = vertical_here.shape[0]
    head_dim = column_keys.shape[-1]
    groups = query_here.shape[1] // (kv_heads * head_dim)
    block_count = length // BS
    query_blocks = query_here.reshape(block_count, BS, kv_heads, groups, head_dim)
    key_blocks = key_ext.reshape(-1, BS, kv_heads, head_dim)
    value_blocks = value_ext.reshape(-1, BS, kv_heads, head_dim)
    head_rows = jnp.arange(kv_heads, dtype=jnp.int32)[:, None]
    score_scale = 1.0 / math.sqrt(head_dim)

    def one_block(block_index):
        query_block = query_first + block_index
        nearby = jnp.clip(query_block - slash_here - ext_first, 0, key_blocks.shape[0] - 1)
        key_rows = jnp.concatenate(
            [key_blocks[nearby, :, head_rows, :], column_keys], axis=1
        ).reshape(kv_heads, -1, head_dim)
        value_rows = jnp.concatenate(
            [value_blocks[nearby, :, head_rows, :], column_values], axis=1
        ).reshape(kv_heads, -1, head_dim)
        active = block_mask(query_block, slash_here, vertical_here)
        return attend_block(query_blocks[block_index], key_rows, value_rows, active, score_scale)

    mixed_rows = lax.map(one_block, jnp.arange(block_count, dtype=jnp.int32))
    return mixed_rows.reshape(length, -1)


def on_device(query_states, key_states, value_states, vertical_blocks, slash_offsets):
    position = lax.axis_index(("seq", "head"))
    length = query_states.shape[0]
    block_count = length // BS
    back_count = -(-((SPAN - 1) * BS) // length)
    near_keys = [key_states]
    near_values = [value_states]
    for distance in range(1, back_count + 1):
        far_key, far_value = passed_along((key_states, value_states), ("seq", "head"), distance)
        near_keys.insert(0, far_key)
        near_values.insert(0, far_value)
    own_keys, own_values = owned_columns(
        key_states, value_states, vertical_blocks, position * block_count
    )
    summed_keys, summed_values = lax.psum((own_keys, own_values), ("seq", "head"))
    return attend_rows(
        query_states,
        jnp.concatenate(near_keys, axis=0),
        jnp.concatenate(near_values, axis=0),
        (position - back_count) * block_count,
        position * block_count,
        summed_keys.astype(jnp.bfloat16),
        summed_values.astype(jnp.bfloat16),
        vertical_blocks,
        slash_offsets,
    )


def solution(mesh):
    in_specs = (
        P(("parts", "seq", "head"), None),
        P(("parts", "seq", "head"), None),
        P(("parts", "seq", "head"), None),
        P("parts", None),
        P("parts", None),
    )
    out_specs = P(("parts", "seq", "head"), None)
    return jax.shard_map(
        on_device, mesh=mesh, in_specs=in_specs, out_specs=out_specs, check_vma=False
    )
```

profile of v0, /device:TPU:8, one launch (start us, length us, event | category | flops | bytes accessed | tf_op | source)
XLA Modules:
  0.0 176.5 jit_solution(5672414072324339948)
XLA Ops:
  0.0 3.5 %collective-permute-start = (bf16[128,1024]{1,0:T(8,128)(2,1)}, bf16[128,1024]{1,0:T(8,128)(2,1)}, u32[]{:S(2)}, u32[]{:S(2)}) collective-permute-start(bf16[128,1024]{1,0:T(8,128)(2,1)} %param.9), channel_id=1, source_target_pairs={{0,4},{1,5},{2,6},{3,7},{4,8},{5,9},{6,10},{7,11},{8,12},{9,13},{1... | collective-permute-start | bytes 786440 | tf_op jit(solution)/shard_map/ppermute | solution.py:15
  3.5 2.6 %collective-permute-start.1 = (bf16[128,1024]{1,0:T(8,128)(2,1)}, bf16[128,1024]{1,0:T(8,128)(2,1)}, u32[]{:S(2)}, u32[]{:S(2)}) collective-permute-start(bf16[128,1024]{1,0:T(8,128)(2,1)} %param.9), channel_id=1, source_target_pairs={{0,3},{1,4},{2,5},{3,6},{4,7},{5,8},{6,9},{7,10},{8,11},{9,12},{10... | collective-permute-start | bytes 786440 | tf_op jit(solution)/shard_map/ppermute | solution.py:15
  6.1 3.5 %collective-permute-start.2 = (bf16[128,1024]{1,0:T(8,128)(2,1)}, bf16[128,1024]{1,0:T(8,128)(2,1)}, u32[]{:S(2)}, u32[]{:S(2)}) collective-permute-start(bf16[128,1024]{1,0:T(8,128)(2,1)} %param.9), channel_id=1, source_target_pairs={{0,2},{1,3},{2,4},{3,5},{4,6},{5,7},{6,8},{7,9},{8,10},{9,11},{10,... | collective-permute-start | bytes 786440 | tf_op jit(solution)/shard_map/ppermute | solution.py:15
  9.5 2.6 %collective-permute-start.3 = (bf16[128,1024]{1,0:T(8,128)(2,1)}, bf16[128,1024]{1,0:T(8,128)(2,1)}, u32[]{:S(2)}, u32[]{:S(2)}) collective-permute-start(bf16[128,1024]{1,0:T(8,128)(2,1)} %param.9), channel_id=1, source_target_pairs={{0,1},{1,2},{2,3},{3,4},{4,5},{5,6},{6,7},{7,8},{8,9},{9,10},{10,1... | collective-permute-start | bytes 786440 | tf_op jit(solution)/shard_map/ppermute | solution.py:15
  12.1 2.1 %collective-permute-start.4 = (bf16[128,1024]{1,0:T(8,128)(2,1)}, bf16[128,1024]{1,0:T(8,128)(2,1)S(1)}, u32[]{:S(2)}, u32[]{:S(2)}) collective-permute-start(bf16[128,1024]{1,0:T(8,128)(2,1)} %param.8), channel_id=1, source_target_pairs={{0,4},{1,5},{2,6},{3,7},{4,8},{5,9},{6,10},{7,11},{8,12},{9,13},{1... | collective-permute-start | bytes 786440 | tf_op jit(solution)/shard_map/ppermute | solution.py:15
  17.9 1.8 %gather_fusion.2 = bf16[48,64,128]{2,1,0:T(8,128)(2,1)} fusion(bf16[2,64,8,128]{3,1,2,0:T(8,128)(2,1)S(1)} %copy.22, s32[48]{0:T(128)S(1)} %reshape.131), kind=kCustom, calls=%fused_computation.2 | custom fusion | bytes 1573248 | tf_op jit(solution)/shard_map/gather | solution.py:65
  23.0 74.7 %all-reduce.2 = (bf16[8,6,64,128]{3,2,1,0:T(8,128)(2,1)}, bf16[8,6,64,128]{3,2,1,0:T(8,128)(2,1)}) all-reduce(f32[8,6,64,128]{3,2,1,0:T(8,128)S(1)} %get-tuple-element.169, f32[8,6,64,128]{3,2,1,0:T(8,128)S(1)} %get-tuple-element.168), channel_id=1, replica_groups=mesh['parts'=2,'seq'=8,'head'=2] {'seq','head'}, use_global_device_ids=true, to_apply=%region_1.2 | all-reduce | flops 786432 | bytes 4718592 | tf_op jit(solution)/shard_map/psum | solution.py:122
  97.8 3.6 %copy.39 = bf16[16,8,64,128]{3,2,1,0:T(8,128)(2,1)} copy(bf16[16,8,64,128]{3,1,2,0:T(8,128)(2,1)} %bitcast.112) | data formatting | bytes 4194304
  101.5 2.3 %collective-permute-start.5 = (bf16[128,1024]{1,0:T(8,128)(2,1)S(1)}, bf16[128,1024]{1,0:T(8,128)(2,1)S(1)}, u32[]{:S(2)}, u32[]{:S(2)}) collective-permute-start(bf16[128,1024]{1,0:T(8,128)(2,1)S(1)} %copy-done.4), channel_id=1, source_target_pairs={{0,3},{1,4},{2,5},{3,6},{4,7},{5,8},{6,9},{7,10},{8,11},{9,12},{10... | collective-permute-start | bytes 786440 | tf_op jit(solution)/shard_map/ppermute | solution.py:15
  104.8 5.5 %collective-permute-start.6 = (bf16[128,1024]{1,0:T(8,128)(2,1)S(1)}, bf16[128,1024]{1,0:T(8,128)(2,1)S(1)}, u32[]{:S(2)}, u32[]{:S(2)}) collective-permute-start(bf16[128,1024]{1,0:T(8,128)(2,1)S(1)} %copy-done.4), channel_id=1, source_target_pairs={{0,2},{1,3},{2,4},{3,5},{4,6},{5,7},{6,8},{7,9},{8,10},{9,11},{10,... | collective-permute-start | bytes 786440 | tf_op jit(solution)/shard_map/ppermute | solution.py:15
  111.2 1.9 %collective-permute-start.7 = (bf16[128,1024]{1,0:T(8,128)(2,1)S(1)}, bf16[128,1024]{1,0:T(8,128)(2,1)S(1)}, u32[]{:S(2)}, u32[]{:S(2)}) collective-permute-start(bf16[128,1024]{1,0:T(8,128)(2,1)S(1)} %copy-done.4), channel_id=1, source_target_pairs={{0,1},{1,2},{2,3},{3,4},{4,5},{5,6},{6,7},{7,8},{8,9},{9,10},{10,1... | collective-permute-start | bytes 786440 | tf_op jit(solution)/shard_map/ppermute | solution.py:15
  116.0 4.0 %collective-permute-done.6 = bf16[128,1024]{1,0:T(8,128)(2,1)S(1)} collective-permute-done((bf16[128,1024]{1,0:T(8,128)(2,1)S(1)}, bf16[128,1024]{1,0:T(8,128)(2,1)S(1)}, u32[]{:S(2)}, u32[]{:S(2)}) %collective-permute-start.6) | collective-permute-done | bytes 262176 | tf_op jit(solution)/shard_map/ppermute | solution.py:15
  123.6 48.7 %while.11 = (s32[]{:T(128)}, bf16[2,64,8,8,128]{4,3,2,1,0:T(8,128)(2,1)}, s32[2]{0:T(128)S(1)}, s32[]{:T(128)}, s32[8,6]{0,1:T(8,128)S(1)}, /*index=5*/s32[]{:T(...) while((s32[]{:T(128)}, ...), condition=%wide.region_6.7_spmd.clone, body=%wide.region_2.6_spmd.clone.sunk | while | flops 1648620800 | bytes 75990280 | solution.py:104
  127.9 2.2 %gather_fusion.1 = bf16[48,64,128]{2,1,0:T(8,128)(2,1)S(1)} fusion(bf16[10,64,8,128]{3,1,2,0:T(8,128)(2,1)} %get-tuple-element.296, s32[48]{0:T(128)S(1)} %reshape.171), kind=kCustom, calls=%fused_computation.1.clone.clone.1 | custom fusion | bytes 1573248 | tf_op jit(solution)/shard_map/while/body/eval_jaxpr/gather | solution.py:96
  130.1 2.8 %pad_maximum_fusion.3 = (bf16[8,12,64,128]{3,2,1,0:T(8,128)(2,1)}, bf16[8,12,64,128]{3,2,1,0:T(8,128)(2,1)S(1)}) fusion(bf16[8,6,64,128]{3,2,1,0:T(8,128)(2,1)} %get-tuple-element.294, bf16[8,6,64,128]{3,2,1,0:T(8,128)(2,1)S(1)} %bitcast.104, bf16[8,6,64,128]{3,2,1,0:T(8,128)(2,1)} %get-tuple-element.297, bf16[8,6,64,128]{3,2,1,0:T(8,128)(2,1)S(1)} %bitcast.105), kind=kLoop, calls=%fused_computation.14.clone.1 | loop fusion | flops 1572864 | bytes 6291456 | tf_op jit(solution)/shard_map/while/body/eval_jaxpr/concatenate | solution.py:98
  136.3 2.9 %fusion.40 = (f32[8,8,64]{2,1,0:T(8,128)S(1)}, f32[8,768,64,8]{1,2,3,0:T(8,128)S(1)}) fusion(pred[8,64,768]{2,1,0:T(8,128)(4,1)S(1)} %pad_add_fusion.2, bf16[8,768,128,1]{2,1,3,0:T(8,128)(2,1)S(1)} %bitcast.103, bf16[1,64,8,8,128]{4,3,2,1,0:T(8,128)(2,1)S(1)} %constant_dynamic-slice_fusion.2), kind=kOutput, calls=%fused_computation.9.clone.1 | convolution fusion | flops 814739456 | bytes 15613952 | tf_op jit(solution)/shard_map/while/body/eval_jaxpr/tgch,gkh->gctk/dot_general | solution.py:37
  139.2 3.2 %fusion.41 = f32[8,8,64]{2,1,0:T(8,128)S(1)} fusion(f32[8,768,64,8]{1,2,3,0:T(8,128)S(1)} %get-tuple-element.255, f32[8,8,64]{2,1,0:T(8,128)S(1)} %get-tuple-element.256, pred[8,64,768]{2,1,0:T(8,128)(4,1)S(1)} %pad_add_fusion.2), kind=kLoop, calls=%fused_computation.7.clone.1 | loop fusion | flops 12578816 | bytes 13008896 | tf_op jit(solution)/shard_map/while/body/eval_jaxpr/reduce_sum | solution.py:43
  142.4 3.8 %fusion.42 = bf16[1,64,8,8,128]{4,1,3,2,0:T(8,128)(2,1)S(1)} fusion(bf16[8,768,128,1]{2,1,3,0:T(8,128)(2,1)S(1)} %bitcast.106, f32[8,768,64,8]{1,2,3,0:T(8,128)S(1)} %get-tuple-element.255, f32[8,8,64]{2,1,0:T(8,128)S(1)} %get-tuple-element.256, pred[8,64,768]{2,1,0:T(8,128)(4,1)S(1)} %pad_add_fusion.2, f32[64,8,8]{0,2,1:T(8,128)S(1)} %bitcast.119), kind=kOutput, calls=%fused_computation.17.clone.1 | convolution fusion | flops 818937856 | bytes 15630336 | tf_op jit(solution)/shard_map/while/body/eval_jaxpr/gctk,gkh->tgch/dot_general | solution.py:45
  152.2 2.2 %gather_fusion.1 = bf16[48,64,128]{2,1,0:T(8,128)(2,1)S(1)} fusion(bf16[10,64,8,128]{3,1,2,0:T(8,128)(2,1)} %get-tuple-element.296, s32[48]{0:T(128)S(1)} %reshape.171), kind=kCustom, calls=%fused_computation.1.clone.clone.1 | custom fusion | bytes 1573248 | tf_op jit(solution)/shard_map/while/body/eval_jaxpr/gather | solution.py:96
  154.4 2.8 %pad_maximum_fusion.3 = (bf16[8,12,64,128]{3,2,1,0:T(8,128)(2,1)}, bf16[8,12,64,128]{3,2,1,0:T(8,128)(2,1)S(1)}) fusion(bf16[8,6,64,128]{3,2,1,0:T(8,128)(2,1)} %get-tuple-element.294, bf16[8,6,64,128]{3,2,1,0:T(8,128)(2,1)S(1)} %bitcast.104, bf16[8,6,64,128]{3,2,1,0:T(8,128)(2,1)} %get-tuple-element.297, bf16[8,6,64,128]{3,2,1,0:T(8,128)(2,1)S(1)} %bitcast.105), kind=kLoop, calls=%fused_computation.14.clone.1 | loop fusion | flops 1572864 | bytes 6291456 | tf_op jit(solution)/shard_map/while/body/eval_jaxpr/concatenate | solution.py:98
  160.6 2.9 %fusion.40 = (f32[8,8,64]{2,1,0:T(8,128)S(1)}, f32[8,768,64,8]{1,2,3,0:T(8,128)S(1)}) fusion(pred[8,64,768]{2,1,0:T(8,128)(4,1)S(1)} %pad_add_fusion.2, bf16[8,768,128,1]{2,1,3,0:T(8,128)(2,1)S(1)} %bitcast.103, bf16[1,64,8,8,128]{4,3,2,1,0:T(8,128)(2,1)S(1)} %constant_dynamic-slice_fusion.2), kind=kOutput, calls=%fused_computation.9.clone.1 | convolution fusion | flops 814739456 | bytes 15613952 | tf_op jit(solution)/shard_map/while/body/eval_jaxpr/tgch,gkh->gctk/dot_general | solution.py:37
  163.5 3.2 %fusion.41 = f32[8,8,64]{2,1,0:T(8,128)S(1)} fusion(f32[8,768,64,8]{1,2,3,0:T(8,128)S(1)} %get-tuple-element.255, f32[8,8,64]{2,1,0:T(8,128)S(1)} %get-tuple-element.256, pred[8,64,768]{2,1,0:T(8,128)(4,1)S(1)} %pad_add_fusion.2), kind=kLoop, calls=%fused_computation.7.clone.1 | loop fusion | flops 12578816 | bytes 13008896 | tf_op jit(solution)/shard_map/while/body/eval_jaxpr/reduce_sum | solution.py:43
  166.7 3.8 %fusion.42 = bf16[1,64,8,8,128]{4,1,3,2,0:T(8,128)(2,1)S(1)} fusion(bf16[8,768,128,1]{2,1,3,0:T(8,128)(2,1)S(1)} %bitcast.106, f32[8,768,64,8]{1,2,3,0:T(8,128)S(1)} %get-tuple-element.255, f32[8,8,64]{2,1,0:T(8,128)S(1)} %get-tuple-element.256, pred[8,64,768]{2,1,0:T(8,128)(4,1)S(1)} %pad_add_fusion.2, f32[64,8,8]{0,2,1:T(8,128)S(1)} %bitcast.119), kind=kOutput, calls=%fused_computation.17.clone.1 | convolution fusion | flops 818937856 | bytes 15630336 | tf_op jit(solution)/shard_map/while/body/eval_jaxpr/gctk,gkh->tgch/dot_general | solution.py:45
  172.3 4.2 %reshape.118 = bf16[128,8192]{1,0:T(8,128)(2,1)} reshape(bf16[2,64,8,8,128]{4,3,2,1,0:T(8,128)(2,1)} %get-tuple-element.72) | data formatting | bytes 4194304 | tf_op jit(solution)/shard_map/reshape | solution.py:105
  (110 shorter events, 28.4 us)
Async XLA Ops:
  0.0 101.5 %collective-permute-start = (bf16[128,1024]{1,0:T(8,128)(2,1)}, bf16[128,1024]{1,0:T(8,128)(2,1)}, u32[]{:S(2)}, u32[]{:S(2)}) collective-permute-start(bf16[128,1024]{1,0:T(8,128)(2,1)} %param.9), channel_id=1, source_target_pairs={{0,4},{1,5},{2,6},{3,7},{4,8},{5,9},{6,10},{7,11},{8,12},{9,13},{1... | collective-permute-start | bytes 786440 | tf_op jit(solution)/shard_map/ppermute | solution.py:15
  3.5 101.3 %collective-permute-start.1 = (bf16[128,1024]{1,0:T(8,128)(2,1)}, bf16[128,1024]{1,0:T(8,128)(2,1)}, u32[]{:S(2)}, u32[]{:S(2)}) collective-permute-start(bf16[128,1024]{1,0:T(8,128)(2,1)} %param.9), channel_id=1, source_target_pairs={{0,3},{1,4},{2,5},{3,6},{4,7},{5,8},{6,9},{7,10},{8,11},{9,12},{10... | collective-permute-start | bytes 786440 | tf_op jit(solution)/shard_map/ppermute | solution.py:15
  6.1 105.2 %collective-permute-start.2 = (bf16[128,1024]{1,0:T(8,128)(2,1)}, bf16[128,1024]{1,0:T(8,128)(2,1)}, u32[]{:S(2)}, u32[]{:S(2)}) collective-permute-start(bf16[128,1024]{1,0:T(8,128)(2,1)} %param.9), channel_id=1, source_target_pairs={{0,2},{1,3},{2,4},{3,5},{4,6},{5,7},{6,8},{7,9},{8,10},{9,11},{10,... | collective-permute-start | bytes 786440 | tf_op jit(solution)/shard_map/ppermute | solution.py:15
  9.5 104.6 %collective-permute-start.3 = (bf16[128,1024]{1,0:T(8,128)(2,1)}, bf16[128,1024]{1,0:T(8,128)(2,1)}, u32[]{:S(2)}, u32[]{:S(2)}) collective-permute-start(bf16[128,1024]{1,0:T(8,128)(2,1)} %param.9), channel_id=1, source_target_pairs={{0,1},{1,2},{2,3},{3,4},{4,5},{5,6},{6,7},{7,8},{8,9},{9,10},{10,1... | collective-permute-start | bytes 786440 | tf_op jit(solution)/shard_map/ppermute | solution.py:15
  12.1 103.0 %collective-permute-start.4 = (bf16[128,1024]{1,0:T(8,128)(2,1)}, bf16[128,1024]{1,0:T(8,128)(2,1)S(1)}, u32[]{:S(2)}, u32[]{:S(2)}) collective-permute-start(bf16[128,1024]{1,0:T(8,128)(2,1)} %param.8), channel_id=1, source_target_pairs={{0,4},{1,5},{2,6},{3,7},{4,8},{5,9},{6,10},{7,11},{8,12},{9,13},{1... | collective-permute-start | bytes 786440 | tf_op jit(solution)/shard_map/ppermute | solution.py:15
  23.0 74.7 %copy-start.5 = (s32[8,6]{1,0:T(8,128)S(1)}, s32[8,6]{1,0:T(8,128)}, u32[]{:S(2)}) copy-start(s32[8,6]{1,0:T(8,128)} %param.10) | copy-start | bytes 580
  97.8 3.6 %copy-start.6 = (s32[8,6]{1,0:T(8,128)S(1)}, s32[8,6]{1,0:T(8,128)}, u32[]{:S(2)}) copy-start(s32[8,6]{1,0:T(8,128)} %param.11) | copy-start | bytes 580
  97.8 3.7 %copy-start.4 = (bf16[128,1024]{1,0:T(8,128)(2,1)S(1)}, bf16[128,1024]{1,0:T(8,128)(2,1)}, u32[]{:S(2)}) copy-start(bf16[128,1024]{1,0:T(8,128)(2,1)} %param.8) | copy-start | bytes 786436
  101.4 13.7 %copy-start.3 = (bf16[128,1024]{1,0:T(8,128)(2,1)S(1)}, bf16[128,1024]{1,0:T(8,128)(2,1)}, u32[]{:S(2)}) copy-start(bf16[128,1024]{1,0:T(8,128)(2,1)} %param.9) | copy-start | bytes 786436
  101.5 14.4 %collective-permute-start.5 = (bf16[128,1024]{1,0:T(8,128)(2,1)S(1)}, bf16[128,1024]{1,0:T(8,128)(2,1)S(1)}, u32[]{:S(2)}, u32[]{:S(2)}) collective-permute-start(bf16[128,1024]{1,0:T(8,128)(2,1)S(1)} %copy-done.4), channel_id=1, source_target_pairs={{0,3},{1,4},{2,5},{3,6},{4,7},{5,8},{6,9},{7,10},{8,11},{9,12},{10... | collective-permute-start | bytes 786440 | tf_op jit(solution)/shard_map/ppermute | solution.py:15
  104.8 15.2 %collective-permute-start.6 = (bf16[128,1024]{1,0:T(8,128)(2,1)S(1)}, bf16[128,1024]{1,0:T(8,128)(2,1)S(1)}, u32[]{:S(2)}, u32[]{:S(2)}) collective-permute-start(bf16[128,1024]{1,0:T(8,128)(2,1)S(1)} %copy-done.4), channel_id=1, source_target_pairs={{0,2},{1,3},{2,4},{3,5},{4,6},{5,7},{6,8},{7,9},{8,10},{9,11},{10,... | collective-permute-start | bytes 786440 | tf_op jit(solution)/shard_map/ppermute | solution.py:15
  111.2 10.5 %collective-permute-start.7 = (bf16[128,1024]{1,0:T(8,128)(2,1)S(1)}, bf16[128,1024]{1,0:T(8,128)(2,1)S(1)}, u32[]{:S(2)}, u32[]{:S(2)}) collective-permute-start(bf16[128,1024]{1,0:T(8,128)(2,1)S(1)} %copy-done.4), channel_id=1, source_target_pairs={{0,1},{1,2},{2,3},{3,4},{4,5},{5,6},{6,7},{7,8},{8,9},{9,10},{10,1... | collective-permute-start | bytes 786440 | tf_op jit(solution)/shard_map/ppermute | solution.py:15
  123.6 4.3 %copy-start.1 = (bf16[10,64,8,128]{3,1,2,0:T(8,128)(2,1)}, bf16[10,64,8,128]{3,1,2,0:T(8,128)(2,1)S(1)}, u32[]{:S(2)}) copy-start(bf16[10,64,8,128]{3,1,2,0:T(8,128)(2,1)S(1)} %get-tuple-element.293) | copy-start | bytes 3932164 | tf_op jit(solution)/shard_map/while
  139.2 3.2 %copy-start = (bf16[8,12,64,128]{3,2,1,0:T(8,128)(2,1)S(1)}, bf16[8,12,64,128]{3,2,1,0:T(8,128)(2,1)}, u32[]{:S(2)}) copy-start(bf16[8,12,64,128]{3,2,1,0:T(8,128)(2,1)} %get-tuple-element.250) | copy-start | bytes 4718596 | tf_op jit(solution)/shard_map/while
  146.3 1.7 copy-start.2
  147.9 4.3 %copy-start.1 = (bf16[10,64,8,128]{3,1,2,0:T(8,128)(2,1)}, bf16[10,64,8,128]{3,1,2,0:T(8,128)(2,1)S(1)}, u32[]{:S(2)}) copy-start(bf16[10,64,8,128]{3,1,2,0:T(8,128)(2,1)S(1)} %get-tuple-element.293) | copy-start | bytes 3932164 | tf_op jit(solution)/shard_map/while
  163.5 3.2 %copy-start = (bf16[8,12,64,128]{3,2,1,0:T(8,128)(2,1)S(1)}, bf16[8,12,64,128]{3,2,1,0:T(8,128)(2,1)}, u32[]{:S(2)}) copy-start(bf16[8,12,64,128]{3,2,1,0:T(8,128)(2,1)} %get-tuple-element.250) | copy-start | bytes 4718596 | tf_op jit(solution)/shard_map/while
  170.6 1.7 copy-start.2
where the time goes:
time: 179 us; the launch traced here: 176 us
  blocking collectives  74.7 us (42%)
  local copies, waits for them, and re-layouts  36.3 us (20%)
  starting transfers between devices  23.9 us (13%)
  other arithmetic  16.2 us (9%)
  matrix products  13.5 us (8%)
  loops' own time  5.8 us (3%)
  waiting for transfers between devices  5.79 us (3%)
    psum x1, blocking collectives, on_device(): lax.psum((own_keys, own_values), ('seq', 'head'))  74.7 us
    ppermute x8, starting transfers between devices, passed_along(): return lax.ppermute(block, axis, route)  23.9 us
    unnamed x25, local copies, waits for them, and re-layouts  12.2 us
    dot_general x2, matrix products, attend_block(): jnp.einsum('gctk,gkh->tgch', rounded, value_rows, preferred_element_type=...  7.69 us
    reduce_sum x2, other arithmetic, attend_block(): row_total = jnp.sum(weights, axis=-1)  6.37 us
    dot_general x2, matrix products, attend_block(): jnp.einsum('tgch,gkh->gctk', query_tile, key_rows, preferred_element_type...  5.83 us
    another operation x1, loops' own time, attend_rows(): mixed_rows = lax.map(one_block, jnp.arange(block_count, dtype=jnp.int32))  5.8 us
    ppermute x8, waiting for transfers between devices, passed_along(): return lax.ppermute(block, axis, route)  5.79 us
  transfers between devices with their start and end apart: 8, of which 2 were waited for; matrix products, arithmetic and copies ran while one was open for 10% of the time, Pallas kernels for 0%

commit v1 on v0

v1 whole, which is shorter than its diff:
```python
import functools
import math

import jax
import jax.numpy as jnp
from jax import lax
from jax.experimental import pallas as pl
from jax.experimental.pallas import tpu as pltpu
from jax.sharding import PartitionSpec as P

BS = 64
SPAN = 8
MASKED = -1e30


def passed_along(block, axis, distance):
    devices = range(lax.axis_size(axis))
    route = [(i - distance, i) for i in devices if i - distance in devices]
    return lax.ppermute(block, axis, route)


def owned_columns(key_here, value_here, vertical_here, first_block):
    block_count = key_here.shape[0] // BS
    kv_heads = vertical_here.shape[0]
    head_dim = key_here.shape[1] // kv_heads
    key_blocks = key_here.reshape(block_count, BS, kv_heads, head_dim)
    value_blocks = value_here.reshape(block_count, BS, kv_heads, head_dim)
    offset = vertical_here - first_block
    inside = ((offset >= 0) & (offset < block_count))[:, :, None, None]
    picked = jnp.clip(offset, 0, block_count - 1)
    head_rows = jnp.arange(kv_heads, dtype=jnp.int32)[:, None]
    zero_fill = jnp.zeros((), key_here.dtype)
    key_cols = jnp.where(inside, key_blocks[picked, :, head_rows, :], zero_fill)
    value_cols = jnp.where(inside, value_blocks[picked, :, head_rows, :], zero_fill)
    return (key_cols, value_cols)


def attention_kernel(
    vertical, slash, q_ref, nk_ref, nv_ref, wk_ref, wv_ref, o_ref, kbuf, vbuf, causal
):
    g = pl.program_id(0)
    position = lax.axis_index(("seq", "head"))
    tokens = q_ref.shape[0]
    head_dim = nk_ref.shape[1]
    groups = q_ref.shape[1] // head_dim
    block_count = tokens // BS
    window_blocks = nk_ref.shape[0] // BS
    back_blocks = window_blocks - block_count
    ns, nv = slash.shape[1], vertical.shape[1]
    window_first = position * block_count - back_blocks
    scale = math.log2(math.e) / math.sqrt(head_dim)

    @pl.when(g == 0)
    def _():
        row = lax.broadcasted_iota(jnp.int32, causal.shape, 0)
        col = lax.broadcasted_iota(jnp.int32, causal.shape, 1)
        causal[...] = jnp.where((col < BS) & (col > row), MASKED, 0.0)
        vbuf[...] = jnp.ones_like(vbuf)

    offsets = [slash[g, m] for m in range(ns)]
    columns = [vertical[g, m] for m in range(nv)]
    ordered = [jnp.int32(0)] + [
        jnp.where(offsets[m] == 0, offsets[0], offsets[m]) for m in range(1, ns)
    ]
    lane = lax.broadcasted_iota(jnp.int32, (1, (ns + nv) * BS), 1)
    for b in range(block_count):
        query_block = position * block_count + b
        own = back_blocks + b
        bias = jnp.zeros(lane.shape, jnp.float32)
        for m in range(ns + nv):
            rows = pl.ds(m * BS, BS)
            if m < ns:
                active = ordered[m] <= query_block
                at = jnp.where(active, own - ordered[m], own)
                at = pl.multiple_of(at * BS, BS)
                key_block = nk_ref[pl.ds(at, BS), :]
                value_block = nv_ref[pl.ds(at, BS), :]
            else:
                j = columns[m - ns]
                active = j <= query_block
                for off in offsets:
                    active = active & (query_block - j != off)
                near = jnp.logical_not(active) | (j >= window_first)
                at = jnp.where(active & near, j - window_first, own)
                at = pl.multiple_of(at * BS, BS)
                far_rows = pl.ds((m - ns) * BS, BS)
                key_block = jnp.where(near, nk_ref[pl.ds(at, BS), :], wk_ref[0, far_rows, :])
                value_block = jnp.where(near, nv_ref[pl.ds(at, BS), :], wv_ref[0, far_rows, :])
            kbuf[b, rows, :] = key_block
            vbuf[b, rows, :head_dim] = value_block
            here = (lane >= m * BS) & (lane < (m + 1) * BS)
            bias = jnp.where(here, jnp.where(active, 0.0, MASKED), bias)
        q_rows = slice(b * BS, (b + 1) * BS)
        query = jnp.concatenate(
            [q_ref[q_rows, c * head_dim : (c + 1) * head_dim] for c in range(groups)], axis=0
        )
        scores = lax.dot_general(
            query, kbuf[b], (((1,), (1,)), ((), ())), preferred_element_type=jnp.float32
        )
        scores = scores * scale + bias
        edge = causal.shape[1]
        edge_mask = jnp.concatenate([causal[...]] * groups, axis=0)
        scores = jnp.concatenate([scores[:, :edge] + edge_mask, scores[:, edge:]], axis=1)
        row_max = jnp.max(scores, axis=-1, keepdims=True)
        weights = jnp.exp2(scores - row_max).astype(jnp.bfloat16)
        mixed = jnp.dot(weights, vbuf[b], preferred_element_type=jnp.float32)
        mixed = (mixed[:, :head_dim] / mixed[:, head_dim:]).astype(o_ref.dtype)
        for c in range(groups):
            o_ref[q_rows, c * head_dim : (c + 1) * head_dim] = mixed[c * BS : (c + 1) * BS]


def attend(query_here, near_keys, near_values, far_keys, far_values, vertical_here, slash_here):
    length, width = query_here.shape
    kv_heads, nv = vertical_here.shape
    ns = slash_here.shape[1]
    head_dim = near_keys.shape[1] // kv_heads
    group_width = width // kv_heads
    block_count = length // BS
    near_spec = pl.BlockSpec((near_keys.shape[0], head_dim), lambda g, *_: (0, g))
    far_spec = pl.BlockSpec((1, nv * BS, head_dim), lambda g, *_: (g, 0, 0))
    row_spec = pl.BlockSpec((length, group_width), lambda g, *_: (0, g))
    slots = (ns + nv) * BS
    return pl.pallas_call(
        attention_kernel,
        grid_spec=pltpu.PrefetchScalarGridSpec(
            num_scalar_prefetch=2,
            grid=(kv_heads,),
            in_specs=[row_spec, near_spec, near_spec, far_spec, far_spec],
            out_specs=row_spec,
            scratch_shapes=[
                pltpu.VMEM((block_count, slots, head_dim), jnp.bfloat16),
                pltpu.VMEM((block_count, slots, 2 * head_dim), jnp.bfloat16),
                pltpu.VMEM((BS, 128), jnp.float32),
            ],
        ),
        out_shape=jax.ShapeDtypeStruct((length, width), query_here.dtype),
        compiler_params=pltpu.CompilerParams(
            dimension_semantics=("arbitrary",), vmem_limit_bytes=40 * 1024 * 1024
        ),
        cost_estimate=pl.CostEstimate(
            flops=4 * length * width * slots,
            bytes_accessed=4 * length * width,
            transcendentals=length * width // head_dim * slots,
        ),
    )(vertical_here, slash_here, query_here, near_keys, near_values, far_keys, far_values)


def on_device(query_states, key_states, value_states, vertical_blocks, slash_offsets):
    position = lax.axis_index(("seq", "head"))
    length = query_states.shape[0]
    block_count = length // BS
    kv_heads, nv = vertical_blocks.shape
    head_dim = key_states.shape[1] // kv_heads
    back_count = -(-((SPAN - 1) * BS) // length)
    near_keys = [key_states]
    near_values = [value_states]
    for distance in range(1, back_count + 1):
        far_key, far_value = passed_along((key_states, value_states), ("seq", "head"), distance)
        near_keys.insert(0, far_key)
        near_values.insert(0, far_value)
    own_keys, own_values = owned_columns(
        key_states, value_states, vertical_blocks, position * block_count
    )
    summed_keys, summed_values = lax.psum((own_keys, own_values), ("seq", "head"))
    return attend(
        query_states,
        jnp.concatenate(near_keys, axis=0),
        jnp.concatenate(near_values, axis=0),
        summed_keys.reshape(kv_heads, nv * BS, head_dim),
        summed_values.reshape(kv_heads, nv * BS, head_dim),
        vertical_blocks,
        slash_offsets,
    )


def solution(mesh):
    in_specs = (
        P(("parts", "seq", "head"), None),
        P(("parts", "seq", "head"), None),
        P(("parts", "seq", "head"), None),
        P("parts", None),
        P("parts", None),
    )
    out_specs = P(("parts", "seq", "head"), None)
    return jax.shard_map(
        on_device, mesh=mesh, in_specs=in_specs, out_specs=out_specs, check_vma=False
    )
```

time: 179 us -> 156 us (0.87)
  blocking collectives: 74.7 us -> 0 us
  waiting for transfers between devices: 5.79 us -> 79 us
  local copies, waits for them, and re-layouts: 36.3 us -> 8.94 us
  Pallas kernels: 0 us -> 16.7 us
  matrix products: 13.5 us -> 0 us
  other arithmetic: 16.2 us -> 2.71 us
  between operations: 0.25 us -> 13.7 us
  starting transfers between devices: 23.9 us -> 32.6 us
  loops' own time: 5.8 us -> 0 us
    psum x1 -> x0, blocking collectives: 74.7 us -> none  [on_device(): lax.psum((own_keys, own_values), ('seq', 'head'))]
    psum x0 -> x1, waiting for transfers between devices: none -> 68.1 us  [on_device(): lax.psum((own_keys, own_values), ('seq', 'head'))]
    pallas_call x0 -> x1, Pallas kernels: none -> 16.7 us  [attend(): pl.pallas_call(attention_kernel, grid_spec=pltpu.PrefetchScalarGridSpec(n...]
    dot_general x4 -> x0, matrix products: 13.5 us -> none  [the longest x2 7.69 us: attend_block(): jnp.einsum('gctk,gkh->tgch', rounded, value_rows, preferred_element_type=...]
    ppermute x8, starting transfers between devices: 23.9 us -> 32.6 us  [passed_along(): return lax.ppermute(block, axis, route)]
    gather x6 -> x2, local copies, waits for them, and re-layouts: 9.68 us -> 1.76 us  [the longest x1 0.88 us: owned_columns(): key_cols = jnp.where(inside, key_blocks[picked, :, head_rows, :], zero_fill)]
    reduce_sum x2 -> x0, other arithmetic: 6.37 us -> none  [attend_block(): row_total = jnp.sum(weights, axis=-1)]
    concatenate x9 -> x1, other arithmetic: 6.65 us -> 0.7 us  [owned_columns(): key_cols = jnp.where(inside, key_blocks[picked, :, head_rows, :], zero_fill)]
  transfers between devices with their start and end apart: 8 -> 9, of which waited for: 2 -> 3; matrix products, arithmetic and copies ran while one was open for 10% -> 5% of each run, Pallas kernels for 0% -> 0%
where the time goes in v1:
time: 156 us; the launch traced here: 154 us
  waiting for transfers between devices  79 us (51%)
  starting transfers between devices  32.6 us (21%)
  Pallas kernels  16.7 us (11%)
  between operations  13.7 us (9%)
  local copies, waits for them, and re-layouts  8.94 us (6%)
  other arithmetic  2.71 us (2%)
    psum x1, waiting for transfers between devices, on_device(): lax.psum((own_keys, own_values), ('seq', 'head'))  68.1 us
    ppermute x8, starting transfers between devices, passed_along(): return lax.ppermute(block, axis, route)  32.6 us
    pallas_call x1, Pallas kernels, attend(): pl.pallas_call(attention_kernel, grid_spec=pltpu.PrefetchScalarGridSpec(n...  16.7 us
    ppermute x8, waiting for transfers between devices, passed_along(): return lax.ppermute(block, axis, route)  10.9 us
    unnamed x24, local copies, waits for them, and re-layouts  6.97 us
  transfers between devices with their start and end apart: 9, of which 3 were waited for; matrix products, arithmetic and copies ran while one was open for 5% of the time, Pallas kernels for 0%

profile of v1, /device:TPU:8, one launch (start us, length us, event | category | flops | bytes accessed | tf_op | source)
XLA Modules:
  0.0 153.6 jit_solution(17437026982883607052)
XLA Ops:
  6.5 1.9 %collective-permute-start.3 = (bf16[128,1024]{1,0:T(8,128)(2,1)}, bf16[128,1024]{1,0:T(8,128)(2,1)S(1)}, u32[]{:S(2)}, u32[]{:S(2)}) collective-permute-start(bf16[128,1024]{1,0:T(8,128)(2,1)} %param.6), channel_id=1, source_target_pairs={{0,1},{1,2},{2,3},{3,4},{4,5},{5,6},{6,7},{7,8},{8,9},{9,10},{10,1... | collective-permute-start | bytes 786440 | tf_op jit(solution)/shard_map/ppermute | solution.py:19
  8.5 3.4 %collective-permute-start.2 = (bf16[128,1024]{1,0:T(8,128)(2,1)}, bf16[128,1024]{1,0:T(8,128)(2,1)S(1)}, u32[]{:S(2)}, u32[]{:S(2)}) collective-permute-start(bf16[128,1024]{1,0:T(8,128)(2,1)} %param.6), channel_id=1, source_target_pairs={{0,2},{1,3},{2,4},{3,5},{4,6},{5,7},{6,8},{7,9},{8,10},{9,11},{10,... | collective-permute-start | bytes 786440 | tf_op jit(solution)/shard_map/ppermute | solution.py:19
  11.9 3.5 %collective-permute-start.6 = (bf16[128,1024]{1,0:T(8,128)(2,1)}, bf16[128,1024]{1,0:T(8,128)(2,1)S(1)}, u32[]{:S(2)}, u32[]{:S(2)}) collective-permute-start(bf16[128,1024]{1,0:T(8,128)(2,1)} %param.7), channel_id=1, source_target_pairs={{0,2},{1,3},{2,4},{3,5},{4,6},{5,7},{6,8},{7,9},{8,10},{9,11},{10,... | collective-permute-start | bytes 786440 | tf_op jit(solution)/shard_map/ppermute | solution.py:19
  15.3 4.1 %collective-permute-start.5 = (bf16[128,1024]{1,0:T(8,128)(2,1)}, bf16[128,1024]{1,0:T(8,128)(2,1)S(1)}, u32[]{:S(2)}, u32[]{:S(2)}) collective-permute-start(bf16[128,1024]{1,0:T(8,128)(2,1)} %param.7), channel_id=1, source_target_pairs={{0,3},{1,4},{2,5},{3,6},{4,7},{5,8},{6,9},{7,10},{8,11},{9,12},{10... | collective-permute-start | bytes 786440 | tf_op jit(solution)/shard_map/ppermute | solution.py:19
  19.4 2.2 %collective-permute-start.4 = (bf16[128,1024]{1,0:T(8,128)(2,1)}, bf16[128,1024]{1,0:T(8,128)(2,1)}, u32[]{:S(2)}, u32[]{:S(2)}) collective-permute-start(bf16[128,1024]{1,0:T(8,128)(2,1)} %param.7), channel_id=1, source_target_pairs={{0,4},{1,5},{2,6},{3,7},{4,8},{5,9},{6,10},{7,11},{8,12},{9,13},{1... | collective-permute-start | bytes 786440 | tf_op jit(solution)/shard_map/ppermute | solution.py:19
  21.7 0.7 compare_and_fusion
  22.4 0.7 fusion.3
  23.1 0.1 reshape.19
  23.2 1.0 copy.11
  24.2 1.0 copy.10
  25.3 0.9 gather_fusion
  26.2 0.9 gather_fusion.1
  27.0 1.3 broadcast_select_fusion
  28.4 1.0 collective-permute-done.4
  29.4 1.9 %collective-permute-start.7 = (bf16[128,1024]{1,0:T(8,128)(2,1)S(1)}, bf16[128,1024]{1,0:T(8,128)(2,1)S(1)}, u32[]{:S(2)}, u32[]{:S(2)}) collective-permute-start(bf16[128,1024]{1,0:T(8,128)(2,1)S(1)} %copy-done.5), channel_id=1, source_target_pairs={{0,1},{1,2},{2,3},{3,4},{4,5},{5,6},{6,7},{7,8},{8,9},{9,10},{10,1... | collective-permute-start | bytes 786440 | tf_op jit(solution)/shard_map/ppermute | solution.py:19
  31.3 1.0 constant_dynamic-update-slice_fusion.9
  32.3 12.1 %collective-permute-start.1 = (bf16[128,1024]{1,0:T(8,128)(2,1)S(1)}, bf16[128,1024]{1,0:T(8,128)(2,1)S(1)}, u32[]{:S(2)}, u32[]{:S(2)}) collective-permute-start(bf16[128,1024]{1,0:T(8,128)(2,1)S(1)} %copy-done.6), channel_id=1, source_target_pairs={{0,3},{1,4},{2,5},{3,6},{4,7},{5,8},{6,9},{7,10},{8,11},{9,12},{10... | collective-permute-start | bytes 786440 | tf_op jit(solution)/shard_map/ppermute | solution.py:19
  44.4 3.5 %collective-permute-start = (bf16[128,1024]{1,0:T(8,128)(2,1)S(1)}, bf16[128,1024]{1,0:T(8,128)(2,1)S(1)}, u32[]{:S(2)}, u32[]{:S(2)}) collective-permute-start(bf16[128,1024]{1,0:T(8,128)(2,1)S(1)} %copy-done.6), channel_id=1, source_target_pairs={{0,4},{1,5},{2,6},{3,7},{4,8},{5,9},{6,10},{7,11},{8,12},{9,13},{1... | collective-permute-start | bytes 786440 | tf_op jit(solution)/shard_map/ppermute | solution.py:19
  48.0 9.9 %collective-permute-done = bf16[128,1024]{1,0:T(8,128)(2,1)S(1)} collective-permute-done((bf16[128,1024]{1,0:T(8,128)(2,1)S(1)}, bf16[128,1024]{1,0:T(8,128)(2,1)S(1)}, u32[]{:S(2)}, u32[]{:S(2)}) %collective-permute-start) | collective-permute-done | bytes 262176 | tf_op jit(solution)/shard_map/ppermute | solution.py:19
  58.1 68.1 %all-reduce.3.cloned.1.call-done = (bf16[8,384,128]{2,1,0:T(8,128)(2,1)}, bf16[8,384,128]{2,1,0:T(8,128)(2,1)}) async-done(((bf16[8,384,128]{2,1,0:T(8,128)(2,1)}, bf16[8,384,128]{2,1,0:T(8,128)(2,1)}), (bf16[8,384,128]{2,1,0:T(8,128)(2,1)}, bf16[8,384,128]{2,1,0:T(8,128)(2,1)})) %all-reduce.3.cloned.1.call-update) | async-done | bytes 1572880 | tf_op jit(solution)/shard_map/psum | solution.py:164
  126.2 1.6 %copy-done.1 = bf16[128,8192]{1,0:T(8,128)(2,1)S(1)} copy-done((bf16[128,8192]{1,0:T(8,128)(2,1)S(1)}, bf16[128,8192]{1,0:T(8,128)(2,1)}, u32[]{:S(2)}) %copy-start.1) | copy-done | bytes 2097176
  127.8 1.1 copy-done.2
  128.9 1.1 copy-done.3
  130.0 16.7 %shard_map.55 = bf16[128,8192]{1,0:T(8,128)(2,1)} custom-call(s32[8,6]{1,0:T(8,128)S(1)} %copy-done, s32[8,6]{1,0:T(8,128)S(1)} %copy-done.4, bf16[128,8192]{1,0:T(8,128)(2,1)S(1)} %copy-done.1, bf16[640,1024]{1,0:T(8,128)(2,1)S(1)} %constant_dynamic-update-slice_fusion.nk_ref, bf16[640,1024]{1,0:T(8,128)(2,1)S(1)} %constant_dynamic-update-slice_fusion.5.nv_ref, ...), custom_call_target="tpu_custom_call" | custom-call | flops 3221225472 | bytes 4194304 | tf_op jit(solution)/shard_map/pallas_call | solution.py:123
  (30 shorter events, 0.3 us)
Async XLA Ops:
  6.5 119.6 %all-reduce.3.cloned.1.call-start = ((), (), s32[]{:S(2)}) async-start(), calls=%async_computation | async-start | bytes 3145728 | tf_op jit(solution)/shard_map/psum | solution.py:164
  6.5 51.5 %collective-permute-start.3 = (bf16[128,1024]{1,0:T(8,128)(2,1)}, bf16[128,1024]{1,0:T(8,128)(2,1)S(1)}, u32[]{:S(2)}, u32[]{:S(2)}) collective-permute-start(bf16[128,1024]{1,0:T(8,128)(2,1)} %param.6), channel_id=1, source_target_pairs={{0,1},{1,2},{2,3},{3,4},{4,5},{5,6},{6,7},{7,8},{8,9},{9,10},{10,1... | collective-permute-start | bytes 786440 | tf_op jit(solution)/shard_map/ppermute | solution.py:19
  8.5 49.5 %collective-permute-start.2 = (bf16[128,1024]{1,0:T(8,128)(2,1)}, bf16[128,1024]{1,0:T(8,128)(2,1)S(1)}, u32[]{:S(2)}, u32[]{:S(2)}) collective-permute-start(bf16[128,1024]{1,0:T(8,128)(2,1)} %param.6), channel_id=1, source_target_pairs={{0,2},{1,3},{2,4},{3,5},{4,6},{5,7},{6,8},{7,9},{8,10},{9,11},{10,... | collective-permute-start | bytes 786440 | tf_op jit(solution)/shard_map/ppermute | solution.py:19
  11.9 32.5 %collective-permute-start.6 = (bf16[128,1024]{1,0:T(8,128)(2,1)}, bf16[128,1024]{1,0:T(8,128)(2,1)S(1)}, u32[]{:S(2)}, u32[]{:S(2)}) collective-permute-start(bf16[128,1024]{1,0:T(8,128)(2,1)} %param.7), channel_id=1, source_target_pairs={{0,2},{1,3},{2,4},{3,5},{4,6},{5,7},{6,8},{7,9},{8,10},{9,11},{10,... | collective-permute-start | bytes 786440 | tf_op jit(solution)/shard_map/ppermute | solution.py:19
  15.3 16.9 %collective-permute-start.5 = (bf16[128,1024]{1,0:T(8,128)(2,1)}, bf16[128,1024]{1,0:T(8,128)(2,1)S(1)}, u32[]{:S(2)}, u32[]{:S(2)}) collective-permute-start(bf16[128,1024]{1,0:T(8,128)(2,1)} %param.7), channel_id=1, source_target_pairs={{0,3},{1,4},{2,5},{3,6},{4,7},{5,8},{6,9},{7,10},{8,11},{9,12},{10... | collective-permute-start | bytes 786440 | tf_op jit(solution)/shard_map/ppermute | solution.py:19
  19.4 9.9 %collective-permute-start.4 = (bf16[128,1024]{1,0:T(8,128)(2,1)}, bf16[128,1024]{1,0:T(8,128)(2,1)}, u32[]{:S(2)}, u32[]{:S(2)}) collective-permute-start(bf16[128,1024]{1,0:T(8,128)(2,1)} %param.7), channel_id=1, source_target_pairs={{0,4},{1,5},{2,6},{3,7},{4,8},{5,9},{6,10},{7,11},{8,12},{9,13},{1... | collective-permute-start | bytes 786440 | tf_op jit(solution)/shard_map/ppermute | solution.py:19
  28.4 1.0 copy-start.5
  28.4 3.9 %copy-start.6 = (bf16[128,1024]{1,0:T(8,128)(2,1)S(1)}, bf16[128,1024]{1,0:T(8,128)(2,1)}, u32[]{:S(2)}) copy-start(bf16[128,1024]{1,0:T(8,128)(2,1)} %param.6) | copy-start | bytes 786436
  29.4 18.5 %collective-permute-start.7 = (bf16[128,1024]{1,0:T(8,128)(2,1)S(1)}, bf16[128,1024]{1,0:T(8,128)(2,1)S(1)}, u32[]{:S(2)}, u32[]{:S(2)}) collective-permute-start(bf16[128,1024]{1,0:T(8,128)(2,1)S(1)} %copy-done.5), channel_id=1, source_target_pairs={{0,1},{1,2},{2,3},{3,4},{4,5},{5,6},{6,7},{7,8},{8,9},{9,10},{10,1... | collective-permute-start | bytes 786440 | tf_op jit(solution)/shard_map/ppermute | solution.py:19
  32.3 25.7 %collective-permute-start.1 = (bf16[128,1024]{1,0:T(8,128)(2,1)S(1)}, bf16[128,1024]{1,0:T(8,128)(2,1)S(1)}, u32[]{:S(2)}, u32[]{:S(2)}) collective-permute-start(bf16[128,1024]{1,0:T(8,128)(2,1)S(1)} %copy-done.6), channel_id=1, source_target_pairs={{0,3},{1,4},{2,5},{3,6},{4,7},{5,8},{6,9},{7,10},{8,11},{9,12},{10... | collective-permute-start | bytes 786440 | tf_op jit(solution)/shard_map/ppermute | solution.py:19
  44.4 13.5 %collective-permute-start = (bf16[128,1024]{1,0:T(8,128)(2,1)S(1)}, bf16[128,1024]{1,0:T(8,128)(2,1)S(1)}, u32[]{:S(2)}, u32[]{:S(2)}) collective-permute-start(bf16[128,1024]{1,0:T(8,128)(2,1)S(1)} %copy-done.6), channel_id=1, source_target_pairs={{0,4},{1,5},{2,6},{3,7},{4,8},{5,9},{6,10},{7,11},{8,12},{9,13},{1... | collective-permute-start | bytes 786440 | tf_op jit(solution)/shard_map/ppermute | solution.py:19
  48.0 78.2 %copy-start = (s32[8,6]{1,0:T(8,128)S(1)}, s32[8,6]{1,0:T(8,128)}, u32[]{:S(2)}) copy-start(s32[8,6]{1,0:T(8,128)} %vertical.1) | copy-start | bytes 580
  48.0 78.2 %copy-start.4 = (s32[8,6]{1,0:T(8,128)S(1)}, s32[8,6]{1,0:T(8,128)}, u32[]{:S(2)}) copy-start(s32[8,6]{1,0:T(8,128)} %slash.1) | copy-start | bytes 580
  126.2 1.6 %copy-start.1 = (bf16[128,8192]{1,0:T(8,128)(2,1)S(1)}, bf16[128,8192]{1,0:T(8,128)(2,1)}, u32[]{:S(2)}) copy-start(bf16[128,8192]{1,0:T(8,128)(2,1)} %q_ref.1) | copy-start | bytes 6291460
  127.8 1.1 copy-start.2
  128.9 1.1 copy-start.3
Sparse Core Ops, SparseCore 0:
  28.5 97.6 all-reduce.2

commit v2 on v1

--- a/solution.py
+++ b/solution.py
@@ -13,26 +13,218 @@
 MASKED = -1e30
 
 
-def passed_along(block, axis, distance):
-    devices = range(lax.axis_size(axis))
-    route = [(i - distance, i) for i in devices if i - distance in devices]
-    return lax.ppermute(block, axis, route)
-
-
-def owned_columns(key_here, value_here, vertical_here, first_block):
-    block_count = key_here.shape[0] // BS
-    kv_heads = vertical_here.shape[0]
-    head_dim = key_here.shape[1] // kv_heads
-    key_blocks = key_here.reshape(block_count, BS, kv_heads, head_dim)
-    value_blocks = value_here.reshape(block_count, BS, kv_heads, head_dim)
-    offset = vertical_here - first_block
-    inside = ((offset >= 0) & (offset < block_count))[:, :, None, None]
-    picked = jnp.clip(offset, 0, block_count - 1)
-    head_rows = jnp.arange(kv_heads, dtype=jnp.int32)[:, None]
-    zero_fill = jnp.zeros((), key_here.dtype)
-    key_cols = jnp.where(inside, key_blocks[picked, :, head_rows, :], zero_fill)
-    value_cols = jnp.where(inside, value_blocks[picked, :, head_rows, :], zero_fill)
-    return (key_cols, value_cols)
+MESH = pl.DeviceIdType.MESH
+
+
+def gather_kernel(
+    lanes, k_ref, v_ref, vertical, nk_ref, nv_ref, wk_ref, wv_ref, parts_k, parts_v, merged, send, recv
+):
+    cores = lax.axis_size("head")
+    levels = lax.axis_size("seq") * cores // lanes
+    me = lax.axis_index(("seq", "head"))
+    level, lane = me // lanes, me % lanes
+    side, core = lane // cores, lane % cores
+    blocks = k_ref.shape[0]
+    share = wk_ref.shape[0] // lanes
+    head_dim = wk_ref.shape[2]
+    nv = vertical.shape[1]
+    across, beside = me + cores * (1 - 2 * side), me + 1 - 2 * core
+    above, below = me + lanes, me - lanes
+    has_above, has_below = level < levels - 1, level > 0
+    always = level >= 0
+
+    def name(device):
+        return {"seq": device // cores, "head": device % cores}
+
+    peers = []
+    for hop in range(1, lanes):
+        peers.append((always, level * lanes + (lane + hop) % lanes))
+    peers += [(has_above, above), (has_below, below)]
+    barrier = pltpu.get_barrier_semaphore()
+    for there, peer in peers:
+
+        @pl.when(there)
+        def _():
+            pl.semaphore_signal(barrier, inc=1, device_id=name(peer), device_id_type=MESH)
+
+    ends = jnp.where(has_above, 1, 0) + jnp.where(has_below, 1, 0)
+    pl.semaphore_wait(barrier, lanes - 1 + ends)
+
+    near = (nk_ref, nv_ref)
+    own = (k_ref, v_ref)
+    far = (wk_ref, wv_ref)
+    parts = (parts_k, parts_v)
+    count = [0]
+
+    class Link:
+        def __init__(self, sends, gets, source, target, device):
+            at = count[0]
+            count[0] += 1
+            self.sends, self.gets = sends, gets
+            self.copy = pltpu.make_async_remote_copy(
+                src_ref=source,
+                dst_ref=target,
+                send_sem=send.at[at],
+                recv_sem=recv.at[at],
+                device_id=name(device),
+                device_id_type=MESH,
+            )
+
+        def start(self):
+            pl.when(self.sends)(lambda: self.copy.start())
+
+        def arrived(self):
+            pl.when(self.gets)(lambda: self.copy.wait_recv())
+
+        def sent(self):
+            pl.when(self.sends)(lambda: self.copy.wait_send())
+
+    def slot(ref, distance):
+        first = (lanes - distance) * blocks
+        return ref.at[first : first + blocks]
+
+    width = share * head_dim
+    links = []
+
+    def link(*args):
+        links.append(Link(*args))
+        return links[-1]
+
+    split, up, out_own, out_far, pair_own, pair_far, pass_low, pass_high = ([] for _ in range(8))
+    mine = pl.ds(lane * blocks, blocks)
+    crossed = (side == 1) | has_below
+    for kv in range(2):
+        for hop in range(1, lanes):
+            to = (lane + hop) % lanes
+            columns = pl.ds(pl.multiple_of(to * width, width), width)
+            split.append(
+                link(
+                    always,
+                    always,
+                    own[kv].at[:, :, columns],
+                    parts[kv].at[mine],
+                    level * lanes + to,
+                )
+            )
+        old = slot(near[kv], lanes)
+        middle = slot(near[kv], cores)
+        first, third = slot(near[kv], 1), slot(near[kv], lanes - 1)
+        up.append(link(has_above, has_below, own[kv], old, above))
+        out_own.append(link(side == 0, side == 1, own[kv], middle, across))
+        out_far.append(
+            link((side == 1) & has_below, (side == 0) & has_below, old, middle, across)
+        )
+        pair_own.append(link(core == 0, core == 1, own[kv], first, beside))
+        pair_far.append(link((core == 1) & has_below, (core == 0) & has_below, old, third, beside))
+        pass_low.append(link((core == 0) & crossed, (core == 1) & crossed, middle, third, beside))
+        pass_high.append(link((core == 1) & crossed, (core == 0) & crossed, middle, first, beside))
+
+    rise, spread_pair, spread_across, spread_last = ([[], []] for _ in range(4))
+    opposite = lane + cores * (1 - 2 * side)
+    for kv in range(2):
+        for h in range(share):
+            here = far[kv].at[lane * share + h]
+            there = far[kv].at[opposite * share + h]
+            rise[kv].append(link(has_above, has_below, merged.at[kv, h], here, above))
+            spread_pair[kv].append(link(has_below, has_below, here, here, beside))
+            spread_across[kv].append(link(has_below, has_below, here, here, across))
+            spread_last[kv].append(link(has_below, has_below, there, there, beside))
+
+    for part in split[: lanes - 1]:
+        part.start()
+    up[0].start()
+    for part in split[lanes - 1 :]:
+        part.start()
+    for kv in range(2):
+        out_own[kv].start()
+        pair_own[kv].start()
+    my_columns = pl.ds(pl.multiple_of(lane * width, width), width)
+    for kv in range(2):
+        parts[kv][mine] = own[kv][:, :, my_columns]
+        slot(near[kv], 0)[...] = own[kv][...]
+
+    @pl.when(level == 0)
+    def _():
+        for kv in range(2):
+            for h in range(share):
+                far[kv][lane * share + h] = jnp.zeros(wk_ref.shape[1:], wk_ref.dtype)
+
+    level_blocks = lanes * blocks
+    for kv in range(2):
+        for part in split[kv * (lanes - 1) : (kv + 1) * (lanes - 1)]:
+            part.arrived()
+        up[kv].arrived()
+        out_far[kv].start()
+        pair_far[kv].start()
+        for h in range(share):
+            rise[kv][h].arrived()
+            spread_across[kv][h].start()
+            spread_pair[kv][h].start()
+            for m in range(nv):
+                at = vertical[lane * share + h, m] - level * level_blocks
+                at_all = jnp.full((BS, head_dim), at, jnp.int32)
+                inside = (at_all >= 0) & (at_all < level_blocks)
+                at = jnp.minimum(jnp.maximum(at, 0), level_blocks - 1)
+                rows = slice(m * BS, (m + 1) * BS)
+                block = parts[kv][at][:, h * head_dim : (h + 1) * head_dim]
+                before = far[kv][lane * share + h, rows, :]
+                merged[kv, h, rows, :] = jnp.where(inside, block, before)
+            rise[kv][h].start()
+        if kv == 0:
+            up[1].start()
+    for kv in range(2):
+        out_own[kv].arrived()
+        out_far[kv].arrived()
+        pass_low[kv].start()
+        pass_high[kv].start()
+    for kv in range(2):
+        for h in range(share):
+            spread_across[kv][h].arrived()
+            spread_last[kv][h].start()
+    for kv in range(2):
+        pair_own[kv].arrived()
+        pair_far[kv].arrived()
+        pass_low[kv].arrived()
+        pass_high[kv].arrived()
+        for h in range(share):
+            spread_pair[kv][h].arrived()
+    for kv in range(2):
+        for h in range(share):
+            spread_last[kv][h].arrived()
+    for each in links:
+        each.sent()
+
+
+def gather(key_here, value_here, vertical_here):
+    tokens, width = key_here.shape
+    kv_heads, nv = vertical_here.shape
+    head_dim = width // kv_heads
+    lanes = -(-((SPAN - 1) * BS) // tokens)
+    share = kv_heads // lanes
+    vmem = pl.BlockSpec(memory_space=pltpu.VMEM)
+    blocks = tokens // BS
+    near = jax.ShapeDtypeStruct(((lanes + 1) * blocks, BS, width), key_here.dtype)
+    far = jax.ShapeDtypeStruct((kv_heads, nv * BS, head_dim), key_here.dtype)
+    copies = 2 * (lanes - 1 + 7 + 4 * share)
+    near_keys, near_values, far_keys, far_values = pl.pallas_call(
+        functools.partial(gather_kernel, lanes),
+        in_specs=[vmem, vmem, pl.BlockSpec(memory_space=pltpu.SMEM)],
+        out_specs=[vmem] * 4,
+        out_shape=[near, near, far, far],
+        scratch_shapes=[
+            pltpu.VMEM((lanes * blocks, BS, share * head_dim), key_here.dtype),
+            pltpu.VMEM((lanes * blocks, BS, share * head_dim), key_here.dtype),
+            pltpu.VMEM((2, share, nv * BS, head_dim), key_here.dtype),
+            pltpu.SemaphoreType.DMA((copies,)),
+            pltpu.SemaphoreType.DMA((copies,)),
+        ],
+        compiler_params=pltpu.CompilerParams(
+            collective_id=0, has_side_effects=True, vmem_limit_bytes=40 * 1024 * 1024
+        ),
+    )(
+        key_here.reshape(blocks, BS, width), value_here.reshape(blocks, BS, width), vertical_here
+    )
+    return near_keys.reshape(-1, width), near_values.reshape(-1, width), far_keys, far_values
 
 
 def attention_kernel(
@@ -146,31 +338,8 @@
 
 
 def on_device(query_states, key_states, value_states, vertical_blocks, slash_offsets):
-    position = lax.axis_index(("seq", "head"))
-    length = query_states.shape[0]
-    block_count = length // BS
-    kv_heads, nv = vertical_blocks.shape
-    head_dim = key_states.shape[1] // kv_heads
-    back_count = -(-((SPAN - 1) * BS) // length)
-    near_keys = [key_states]
-    near_values = [value_states]
-    for distance in range(1, back_count + 1):
-        far_key, far_value = passed_along((key_states, value_states), ("seq", "head"), distance)
-        near_keys.insert(0, far_key)
-        near_values.insert(0, far_value)
-    own_keys, own_values = owned_columns(
-        key_states, value_states, vertical_blocks, position * block_count
-    )
-    summed_keys, summed_values = lax.psum((own_keys, own_values), ("seq", "head"))
-    return attend(
-        query_states,
-        jnp.concatenate(near_keys, axis=0),
-        jnp.concatenate(near_values, axis=0),
-        summed_keys.reshape(kv_heads, nv * BS, head_dim),
-        summed_values.reshape(kv_heads, nv * BS, head_dim),
-        vertical_blocks,
-        slash_offsets,
-    )
+    gathered = gather(key_states, value_states, vertical_blocks)
+    return attend(query_states, *gathered, vertical_blocks, slash_offsets)
 
 
 def solution(mesh):

time: 156 us -> 60.3 us (0.39)
  the two profiles are of different devices: /device:TPU:8 before, /device:TPU:29 now
where the time goes in v2:
time: 60.3 us; the launch traced here: 60 us
  Pallas kernels  54.4 us (90%)
  local copies, waits for them, and re-layouts  5.54 us (9%)
    pallas_call x1, Pallas kernels, gather(): pl.pallas_call(functools.partial(gather_kernel, lanes), in_specs=[vmem, v...  37.6 us
    pallas_call x1, Pallas kernels, attend(): pl.pallas_call(attention_kernel, grid_spec=pltpu.PrefetchScalarGridSpec(n...  16.8 us
    unnamed x12, local copies, waits for them, and re-layouts  5.54 us

profile of v2, /device:TPU:29, one launch (start us, length us, event | category | flops | bytes accessed | tf_op | source)
XLA Modules:
  0.0 60.0 jit_solution(12123240673000962393)
XLA Ops:
  0.0 0.0 copy-start
  0.0 0.9 %copy-done = bf16[128,1024]{1,0:T(8,128)(2,1)S(1)} copy-done((bf16[128,1024]{1,0:T(8,128)(2,1)S(1)}, bf16[128,1024]{1,0:T(8,128)(2,1)}, u32[]{:S(2)}) %copy-start) | copy-done | bytes 262168
  1.0 0.0 copy-start.1
  1.0 0.9 %copy-done.1 = bf16[128,1024]{1,0:T(8,128)(2,1)S(1)} copy-done((bf16[128,1024]{1,0:T(8,128)(2,1)S(1)}, bf16[128,1024]{1,0:T(8,128)(2,1)}, u32[]{:S(2)}) %copy-start.1) | copy-done | bytes 262168
  1.9 0.0 copy-start.2
  1.9 0.7 %copy-done.2 = s32[8,6]{1,0:T(8,128)S(1)} copy-done((s32[8,6]{1,0:T(8,128)S(1)}, s32[8,6]{1,0:T(8,128)}, u32[]{:S(2)}) %copy-start.2) | copy-done | bytes 216
  2.6 37.6 %shard_map.55 = (bf16[10,64,1024]{2,1,0:T(8,128)(2,1)S(1)}, bf16[10,64,1024]{2,1,0:T(8,128)(2,1)S(1)}, bf16[8,384,128]{2,1,0:T(8,128)(2,1)S(1)}, bf16[8,384,128]{2,1,0:T(8,128)(2,1)S(1)}) custom-call(bf16[2,64,1024]{2,1,0:T(8,128)(2,1)S(1)} %bitcast.4, bf16[2,64,1024]{2,1,0:T(8,128)(2,1)S(1)} %bitcast.5, s32[8,6]{1,0:T(8,128)S(1)} %copy-done.2), custom_call_target="tpu_custom_call" | custom-call | tf_op jit(solution)/shard_map/pallas_call | solution.py:209
  40.2 0.0 copy-start.3
  40.2 0.7 %copy-done.3 = s32[8,6]{1,0:T(8,128)S(1)} copy-done((s32[8,6]{1,0:T(8,128)S(1)}, s32[8,6]{1,0:T(8,128)}, u32[]{:S(2)}) %copy-start.3) | copy-done | bytes 216
  40.9 0.0 copy-start.4
  40.9 1.6 %copy-done.4 = bf16[128,8192]{1,0:T(8,128)(2,1)S(1)} copy-done((bf16[128,8192]{1,0:T(8,128)(2,1)S(1)}, bf16[128,8192]{1,0:T(8,128)(2,1)}, u32[]{:S(2)}) %copy-start.4) | copy-done | bytes 2097176
  42.4 0.0 copy-start.5
  42.4 0.7 %copy-done.5 = s32[8,6]{1,0:T(8,128)S(1)} copy-done((s32[8,6]{1,0:T(8,128)S(1)}, s32[8,6]{1,0:T(8,128)}, u32[]{:S(2)}) %copy-start.5) | copy-done | bytes 216
  43.1 16.8 %shard_map.56 = bf16[128,8192]{1,0:T(8,128)(2,1)} custom-call(s32[8,6]{1,0:T(8,128)S(1)} %copy-done.3, s32[8,6]{1,0:T(8,128)S(1)} %copy-done.5, bf16[128,8192]{1,0:T(8,128)(2,1)S(1)} %copy-done.4, bf16[640,1024]{1,0:T(8,128)(2,1)S(1)} %bitcast.6, bf16[640,1024]{1,0:T(8,128)(2,1)S(1)} %bitcast.7, bf16[8,384,128]{2,1,0:T(8,128)(2,1)S(1)} %get-tuple-element.11.wk_ref, ...), custom_call_target="tpu_custom_call" | custom-call | flops 3221225472 | bytes 4194304 | tf_op jit(solution)/shard_map/pallas_call | solution.py:315
Async XLA Ops:
  0.0 0.9 %copy-start = (bf16[128,1024]{1,0:T(8,128)(2,1)S(1)}, bf16[128,1024]{1,0:T(8,128)(2,1)}, u32[]{:S(2)}) copy-start(bf16[128,1024]{1,0:T(8,128)(2,1)} %param.6) | copy-start | bytes 786436
  1.0 0.9 %copy-start.1 = (bf16[128,1024]{1,0:T(8,128)(2,1)S(1)}, bf16[128,1024]{1,0:T(8,128)(2,1)}, u32[]{:S(2)}) copy-start(bf16[128,1024]{1,0:T(8,128)(2,1)} %param.7) | copy-start | bytes 786436
  1.9 0.7 %copy-start.2 = (s32[8,6]{1,0:T(8,128)S(1)}, s32[8,6]{1,0:T(8,128)}, u32[]{:S(2)}) copy-start(s32[8,6]{1,0:T(8,128)} %vertical.3) | copy-start | bytes 580
  40.2 0.7 %copy-start.3 = (s32[8,6]{1,0:T(8,128)S(1)}, s32[8,6]{1,0:T(8,128)}, u32[]{:S(2)}) copy-start(s32[8,6]{1,0:T(8,128)} %vertical.3) | copy-start | bytes 580
  40.9 1.6 %copy-start.4 = (bf16[128,8192]{1,0:T(8,128)(2,1)S(1)}, bf16[128,8192]{1,0:T(8,128)(2,1)}, u32[]{:S(2)}) copy-start(bf16[128,8192]{1,0:T(8,128)(2,1)} %q_ref.1) | copy-start | bytes 6291460
  42.4 0.7 %copy-start.5 = (s32[8,6]{1,0:T(8,128)S(1)}, s32[8,6]{1,0:T(8,128)}, u32[]{:S(2)}) copy-start(s32[8,6]{1,0:T(8,128)} %slash.1) | copy-start | bytes 580

commit v3 on v2

--- a/solution.py
+++ b/solution.py
@@ -70,11 +70,11 @@
                 device_id_type=MESH,
             )
 
-        def start(self):
-            pl.when(self.sends)(lambda: self.copy.start())
-
-        def arrived(self):
-            pl.when(self.gets)(lambda: self.copy.wait_recv())
+        def start(self, when=True):
+            pl.when(self.sends & when)(lambda: self.copy.start())
+
+        def arrived(self, when=True):
+            pl.when(self.gets & when)(lambda: self.copy.wait_recv())
 
         def sent(self):
             pl.when(self.sends)(lambda: self.copy.wait_send())
@@ -135,6 +135,7 @@
     up[0].start()
     for part in split[lanes - 1 :]:
         part.start()
+    up[1].start(has_below)
     for kv in range(2):
         out_own[kv].start()
         pair_own[kv].start()
@@ -150,16 +151,21 @@
                 far[kv][lane * share + h] = jnp.zeros(wk_ref.shape[1:], wk_ref.dtype)
 
     level_blocks = lanes * blocks
-    for kv in range(2):
-        for part in split[kv * (lanes - 1) : (kv + 1) * (lanes - 1)]:
-            part.arrived()
-        up[kv].arrived()
-        out_far[kv].start()
-        pair_far[kv].start()
+    def pass_on(kv, when=True):
+        up[kv].arrived(when)
+        out_far[kv].start(when)
+        pair_far[kv].start(when)
+
+    for part in split[: lanes - 1]:
+        part.arrived()
+    pass_on(0)
+    pass_on(1, level > 1)
+    for kv in range(2):
+        if kv == 1:
+            for part in split[lanes - 1 :]:
+                part.arrived()
         for h in range(share):
             rise[kv][h].arrived()
-            spread_across[kv][h].start()
-            spread_pair[kv][h].start()
             for m in range(nv):
                 at = vertical[lane * share + h, m] - level * level_blocks
                 at_all = jnp.full((BS, head_dim), at, jnp.int32)
@@ -170,8 +176,10 @@
                 before = far[kv][lane * share + h, rows, :]
                 merged[kv, h, rows, :] = jnp.where(inside, block, before)
             rise[kv][h].start()
-        if kv == 0:
-            up[1].start()
+            spread_across[kv][h].start()
+            spread_pair[kv][h].start()
+    up[1].start(level == 0)
+    pass_on(1, level == 1)
     for kv in range(2):
         out_own[kv].arrived()
         out_far[kv].arrived()
@@ -219,7 +227,7 @@
             pltpu.SemaphoreType.DMA((copies,)),
         ],
         compiler_params=pltpu.CompilerParams(
-            collective_id=0, has_side_effects=True, vmem_limit_bytes=40 * 1024 * 1024
+            collective_id=0, has_side_effects=True, vmem_limit_bytes=16 * 1024 * 1024
         ),
     )(
         key_here.reshape(blocks, BS, width), value_here.reshape(blocks, BS, width), vertical_here
@@ -228,7 +236,7 @@
 
 
 def attention_kernel(
-    vertical, slash, q_ref, nk_ref, nv_ref, wk_ref, wv_ref, o_ref, kbuf, vbuf, causal
+    vertical, slash, q_ref, nk_ref, nv_ref, wk_ref, wv_ref, o_ref, kbuf, vbuf
 ):
     g = pl.program_id(0)
     position = lax.axis_index(("seq", "head"))
@@ -242,23 +250,25 @@
     window_first = position * block_count - back_blocks
     scale = math.log2(math.e) / math.sqrt(head_dim)
 
+    row = lax.broadcasted_iota(jnp.int32, (BS, head_dim), 0)
+    col = lax.broadcasted_iota(jnp.int32, (BS, head_dim), 1)
+    token = jnp.where(row == col, 1.0, 0.0).astype(kbuf.dtype)
+
     @pl.when(g == 0)
     def _():
-        row = lax.broadcasted_iota(jnp.int32, causal.shape, 0)
-        col = lax.broadcasted_iota(jnp.int32, causal.shape, 1)
-        causal[...] = jnp.where((col < BS) & (col > row), MASKED, 0.0)
         vbuf[...] = jnp.ones_like(vbuf)
+        later = jnp.where((col < BS) & (row > col), MASKED, 0.0).astype(kbuf.dtype)
+        for b in range(block_count):
+            kbuf[b, :BS, head_dim:] = later
 
     offsets = [slash[g, m] for m in range(ns)]
     columns = [vertical[g, m] for m in range(nv)]
     ordered = [jnp.int32(0)] + [
         jnp.where(offsets[m] == 0, offsets[0], offsets[m]) for m in range(1, ns)
     ]
-    lane = lax.broadcasted_iota(jnp.int32, (1, (ns + nv) * BS), 1)
     for b in range(block_count):
         query_block = position * block_count + b
         own = back_blocks + b
-        bias = jnp.zeros(lane.shape, jnp.float32)
         for m in range(ns + nv):
             rows = pl.ds(m * BS, BS)
             if m < ns:
@@ -278,23 +288,24 @@
                 far_rows = pl.ds((m - ns) * BS, BS)
                 key_block = jnp.where(near, nk_ref[pl.ds(at, BS), :], wk_ref[0, far_rows, :])
                 value_block = jnp.where(near, nv_ref[pl.ds(at, BS), :], wv_ref[0, far_rows, :])
-            kbuf[b, rows, :] = key_block
+            kbuf[b, rows, :head_dim] = key_block
             vbuf[b, rows, :head_dim] = value_block
-            here = (lane >= m * BS) & (lane < (m + 1) * BS)
-            bias = jnp.where(here, jnp.where(active, 0.0, MASKED), bias)
+            if m > 0:
+                hidden = jnp.full((BS, head_dim), jnp.where(active, 0.0, MASKED), jnp.float32)
+                kbuf[b, rows, head_dim:] = hidden.astype(kbuf.dtype)
         q_rows = slice(b * BS, (b + 1) * BS)
         query = jnp.concatenate(
-            [q_ref[q_rows, c * head_dim : (c + 1) * head_dim] for c in range(groups)], axis=0
+            [
+                jnp.concatenate([q_ref[q_rows, c * head_dim : (c + 1) * head_dim], token], axis=1)
+                for c in range(groups)
+            ],
+            axis=0,
         )
         scores = lax.dot_general(
             query, kbuf[b], (((1,), (1,)), ((), ())), preferred_element_type=jnp.float32
         )
-        scores = scores * scale + bias
-        edge = causal.shape[1]
-        edge_mask = jnp.concatenate([causal[...]] * groups, axis=0)
-        scores = jnp.concatenate([scores[:, :edge] + edge_mask, scores[:, edge:]], axis=1)
         row_max = jnp.max(scores, axis=-1, keepdims=True)
-        weights = jnp.exp2(scores - row_max).astype(jnp.bfloat16)
+        weights = jnp.exp2((scores - row_max) * scale).astype(jnp.bfloat16)
         mixed = jnp.dot(weights, vbuf[b], preferred_element_type=jnp.float32)
         mixed = (mixed[:, :head_dim] / mixed[:, head_dim:]).astype(o_ref.dtype)
         for c in range(groups):
@@ -320,14 +331,13 @@
             in_specs=[row_spec, near_spec, near_spec, far_spec, far_spec],
             out_specs=row_spec,
             scratch_shapes=[
-                pltpu.VMEM((block_count, slots, head_dim), jnp.bfloat16),
                 pltpu.VMEM((block_count, slots, 2 * head_dim), jnp.bfloat16),
-                pltpu.VMEM((BS, 128), jnp.float32),
+                pltpu.VMEM((block_count, slots, 2 * head_dim), jnp.bfloat16),
             ],
         ),
         out_shape=jax.ShapeDtypeStruct((length, width), query_here.dtype),
         compiler_params=pltpu.CompilerParams(
-            dimension_semantics=("arbitrary",), vmem_limit_bytes=40 * 1024 * 1024
+            dimension_semantics=("arbitrary",), vmem_limit_bytes=24 * 1024 * 1024
         ),
         cost_estimate=pl.CostEstimate(
             flops=4 * length * width * slots,

time: 60.3 us -> 56 us (0.929)
  the two profiles are of different devices: /device:TPU:29 before, /device:TPU:8 now
where the time goes in v3:
time: 56 us; the launch traced here: 55.1 us
  Pallas kernels  49.5 us (88%)
  local copies, waits for them, and re-layouts  5.54 us (10%)
    pallas_call x1, Pallas kernels, gather(): pl.pallas_call(functools.partial(gather_kernel, lanes), in_specs=[vmem, v...  33.1 us
    pallas_call x1, Pallas kernels, attend(): pl.pallas_call(attention_kernel, grid_spec=pltpu.PrefetchScalarGridSpec(n...  16.4 us
    unnamed x12, local copies, waits for them, and re-layouts  5.54 us

profile of v3, /device:TPU:8, one launch (start us, length us, event | category | flops | bytes accessed | tf_op | source)
XLA Modules:
  0.0 55.1 jit_solution(4986739666307340889)
XLA Ops:
  0.0 0.0 copy-start
  0.0 0.9 %copy-done = bf16[128,1024]{1,0:T(8,128)(2,1)S(1)} copy-done((bf16[128,1024]{1,0:T(8,128)(2,1)S(1)}, bf16[128,1024]{1,0:T(8,128)(2,1)}, u32[]{:S(2)}) %copy-start) | copy-done | bytes 262168
  1.0 0.0 copy-start.1
  1.0 0.9 %copy-done.1 = bf16[128,1024]{1,0:T(8,128)(2,1)S(1)} copy-done((bf16[128,1024]{1,0:T(8,128)(2,1)S(1)}, bf16[128,1024]{1,0:T(8,128)(2,1)}, u32[]{:S(2)}) %copy-start.1) | copy-done | bytes 262168
  1.9 0.0 copy-start.2
  1.9 0.7 %copy-done.2 = s32[8,6]{1,0:T(8,128)S(1)} copy-done((s32[8,6]{1,0:T(8,128)S(1)}, s32[8,6]{1,0:T(8,128)}, u32[]{:S(2)}) %copy-start.2) | copy-done | bytes 216
  2.6 33.1 %shard_map.55 = (bf16[10,64,1024]{2,1,0:T(8,128)(2,1)S(1)}, bf16[10,64,1024]{2,1,0:T(8,128)(2,1)S(1)}, bf16[8,384,128]{2,1,0:T(8,128)(2,1)S(1)}, bf16[8,384,128]{2,1,0:T(8,128)(2,1)S(1)}) custom-call(bf16[2,64,1024]{2,1,0:T(8,128)(2,1)S(1)} %bitcast.4, bf16[2,64,1024]{2,1,0:T(8,128)(2,1)S(1)} %bitcast.5, s32[8,6]{1,0:T(8,128)S(1)} %copy-done.2), custom_call_target="tpu_custom_call" | custom-call | tf_op jit(solution)/shard_map/pallas_call | solution.py:217
  35.7 0.0 copy-start.3
  35.7 0.7 %copy-done.3 = s32[8,6]{1,0:T(8,128)S(1)} copy-done((s32[8,6]{1,0:T(8,128)S(1)}, s32[8,6]{1,0:T(8,128)}, u32[]{:S(2)}) %copy-start.3) | copy-done | bytes 216
  36.4 0.0 copy-start.4
  36.4 1.6 %copy-done.4 = bf16[128,8192]{1,0:T(8,128)(2,1)S(1)} copy-done((bf16[128,8192]{1,0:T(8,128)(2,1)S(1)}, bf16[128,8192]{1,0:T(8,128)(2,1)}, u32[]{:S(2)}) %copy-start.4) | copy-done | bytes 2097176
  38.0 0.0 copy-start.5
  38.0 0.7 %copy-done.5 = s32[8,6]{1,0:T(8,128)S(1)} copy-done((s32[8,6]{1,0:T(8,128)S(1)}, s32[8,6]{1,0:T(8,128)}, u32[]{:S(2)}) %copy-start.5) | copy-done | bytes 216
  38.7 16.4 %shard_map.56 = bf16[128,8192]{1,0:T(8,128)(2,1)} custom-call(s32[8,6]{1,0:T(8,128)S(1)} %copy-done.3, s32[8,6]{1,0:T(8,128)S(1)} %copy-done.5, bf16[128,8192]{1,0:T(8,128)(2,1)S(1)} %copy-done.4, bf16[640,1024]{1,0:T(8,128)(2,1)S(1)} %bitcast.6, bf16[640,1024]{1,0:T(8,128)(2,1)S(1)} %bitcast.7, bf16[8,384,128]{2,1,0:T(8,128)(2,1)S(1)} %get-tuple-element.11.wk_ref, ...), custom_call_target="tpu_custom_call" | custom-call | flops 3221225472 | bytes 4194304 | tf_op jit(solution)/shard_map/pallas_call | solution.py:326
Async XLA Ops:
  0.0 0.9 %copy-start = (bf16[128,1024]{1,0:T(8,128)(2,1)S(1)}, bf16[128,1024]{1,0:T(8,128)(2,1)}, u32[]{:S(2)}) copy-start(bf16[128,1024]{1,0:T(8,128)(2,1)} %param.6) | copy-start | bytes 786436
  1.0 0.9 %copy-start.1 = (bf16[128,1024]{1,0:T(8,128)(2,1)S(1)}, bf16[128,1024]{1,0:T(8,128)(2,1)}, u32[]{:S(2)}) copy-start(bf16[128,1024]{1,0:T(8,128)(2,1)} %param.7) | copy-start | bytes 786436
  1.9 0.7 %copy-start.2 = (s32[8,6]{1,0:T(8,128)S(1)}, s32[8,6]{1,0:T(8,128)}, u32[]{:S(2)}) copy-start(s32[8,6]{1,0:T(8,128)} %vertical.3) | copy-start | bytes 580
  35.7 0.7 %copy-start.3 = (s32[8,6]{1,0:T(8,128)S(1)}, s32[8,6]{1,0:T(8,128)}, u32[]{:S(2)}) copy-start(s32[8,6]{1,0:T(8,128)} %vertical.3) | copy-start | bytes 580
  36.4 1.6 %copy-start.4 = (bf16[128,8192]{1,0:T(8,128)(2,1)S(1)}, bf16[128,8192]{1,0:T(8,128)(2,1)}, u32[]{:S(2)}) copy-start(bf16[128,8192]{1,0:T(8,128)(2,1)} %q_ref.1) | copy-start | bytes 6291460
  38.0 0.7 %copy-start.5 = (s32[8,6]{1,0:T(8,128)S(1)}, s32[8,6]{1,0:T(8,128)}, u32[]{:S(2)}) copy-start(s32[8,6]{1,0:T(8,128)} %slash.1) | copy-start | bytes 580

commit v4 on v3

v4 whole, which is shorter than its diff:
```python
import functools
import math

import jax
import jax.numpy as jnp
from jax import lax
from jax.experimental import pallas as pl
from jax.experimental.pallas import tpu as pltpu
from jax.sharding import PartitionSpec as P

BS = 64
SPAN = 8
MASKED = -1e30


MESH = pl.DeviceIdType.MESH


def fused_kernel(
    lanes,
    q_hbm,
    k_ref,
    v_ref,
    vertical,
    slash,
    o_ref,
    q_ref,
    nk_ref,
    nv_ref,
    wk_ref,
    wv_ref,
    parts_k,
    parts_v,
    merged,
    kbuf,
    vbuf,
    top,
    total,
    mixed,
    send,
    recv,
    local,
):
    cores = lax.axis_size("head")
    levels = lax.axis_size("seq") * cores // lanes
    me = lax.axis_index(("seq", "head"))
    level, lane = me // lanes, me % lanes
    side, core = lane // cores, lane % cores
    blocks = k_ref.shape[0]
    share = wk_ref.shape[0] // lanes
    head_dim = wk_ref.shape[2]
    nv = vertical.shape[1]
    across, beside = me + cores * (1 - 2 * side), me + 1 - 2 * core
    above, below = me + lanes, me - lanes
    has_above, has_below = level < levels - 1, level > 0
    always = level >= 0

    def name(device):
        return {"seq": device // cores, "head": device % cores}

    peers = []
    for hop in range(1, lanes):
        peers.append((always, level * lanes + (lane + hop) % lanes))
    peers += [(has_above, above), (has_below, below)]
    barrier = pltpu.get_barrier_semaphore()
    for there, peer in peers:

        @pl.when(there)
        def _():
            pl.semaphore_signal(barrier, inc=1, device_id=name(peer), device_id_type=MESH)

    ends = jnp.where(has_above, 1, 0) + jnp.where(has_below, 1, 0)
    pl.semaphore_wait(barrier, lanes - 1 + ends)

    near = (nk_ref, nv_ref)
    own = (k_ref, v_ref)
    far = (wk_ref, wv_ref)
    parts = (parts_k, parts_v)
    count = [0]

    class Link:
        def __init__(self, sends, gets, source, target, device):
            at = count[0]
            count[0] += 1
            self.sends, self.gets = sends, gets
            self.copy = pltpu.make_async_remote_copy(
                src_ref=source,
                dst_ref=target,
                send_sem=send.at[at],
                recv_sem=recv.at[at],
                device_id=name(device),
                device_id_type=MESH,
            )

        def start(self, when=True):
            pl.when(self.sends & when)(lambda: self.copy.start())

        def arrived(self, when=True):
            pl.when(self.gets & when)(lambda: self.copy.wait_recv())

        def sent(self):
            pl.when(self.sends)(lambda: self.copy.wait_send())

    def slot(ref, distance):
        first = (lanes - distance) * blocks
        return ref.at[first : first + blocks]

    width = share * head_dim
    links = []

    def link(*args):
        links.append(Link(*args))
        return links[-1]

    split, up, out_own, out_far, pair_own, pair_far, pass_low, pass_high = ([] for _ in range(8))
    mine = pl.ds(lane * blocks, blocks)
    crossed = (side == 1) | has_below
    for kv in range(2):
        for hop in range(1, lanes):
            to = (lane + hop) % lanes
            columns = pl.ds(pl.multiple_of(to * width, width), width)
            split.append(
                link(
                    always,
                    always,
                    own[kv].at[:, :, columns],
                    parts[kv].at[mine],
                    level * lanes + to,
                )
            )
        old = slot(near[kv], lanes)
        middle = slot(near[kv], cores)
        first, third = slot(near[kv], 1), slot(near[kv], lanes - 1)
        up.append(link(has_above, has_below, own[kv], old, above))
        out_own.append(link(side == 0, side == 1, own[kv], middle, across))
        out_far.append(
            link((side == 1) & has_below, (side == 0) & has_below, old, middle, across)
        )
        pair_own.append(link(core == 0, core == 1, own[kv], first, beside))
        pair_far.append(link((core == 1) & has_below, (core == 0) & has_below, old, third, beside))
        pass_low.append(link((core == 0) & crossed, (core == 1) & crossed, middle, third, beside))
        pass_high.append(link((core == 1) & crossed, (core == 0) & crossed, middle, first, beside))

    rise, spread_pair, spread_across, spread_last = ([[], []] for _ in range(4))
    opposite = lane + cores * (1 - 2 * side)
    for kv in range(2):
        for h in range(share):
            here = far[kv].at[lane * share + h]
            there = far[kv].at[opposite * share + h]
            rise[kv].append(link(has_above, has_below, merged.at[kv, h], here, above))
            spread_pair[kv].append(link(has_below, has_below, here, here, beside))
            spread_across[kv].append(link(has_below, has_below, here, here, across))
            spread_last[kv].append(link(has_below, has_below, there, there, beside))

    for part in split[: lanes - 1]:
        part.start()
    up[0].start()
    for part in split[lanes - 1 :]:
        part.start()
    up[1].start(has_below)
    for kv in range(2):
        out_own[kv].start()
        pair_own[kv].start()
    my_columns = pl.ds(pl.multiple_of(lane * width, width), width)
    kept = []
    for kv in range(2):
        kept.append((own[kv].at[:, :, my_columns], parts[kv].at[mine]))
        kept.append((own[kv], slot(near[kv], 0)))
    kept.append((q_hbm, q_ref))
    kept = [
        pltpu.make_async_copy(source, target, local.at[i])
        for i, (source, target) in enumerate(kept)
    ]
    for copy in kept:
        copy.start()

    @pl.when(level == 0)
    def _():
        for kv in range(2):
            for h in range(share):
                far[kv][lane * share + h] = jnp.zeros(wk_ref.shape[1:], wk_ref.dtype)

    level_blocks = lanes * blocks
    def pass_on(kv, when=True):
        up[kv].arrived(when)
        out_far[kv].start(when)
        pair_far[kv].start(when)

    for part in split[: lanes - 1]:
        part.arrived()
    for copy in kept:
        copy.wait()
    pass_on(0)
    pass_on(1, level > 1)
    for kv in range(2):
        if kv == 1:
            for part in split[lanes - 1 :]:
                part.arrived()
        for h in range(share):
            rise[kv][h].arrived()
            for m in range(nv):
                at = vertical[lane * share + h, m] - level * level_blocks
                at_all = jnp.full((BS, head_dim), at, jnp.int32)
                inside = (at_all >= 0) & (at_all < level_blocks)
                at = jnp.minimum(jnp.maximum(at, 0), level_blocks - 1)
                rows = slice(m * BS, (m + 1) * BS)
                block = parts[kv][at][:, h * head_dim : (h + 1) * head_dim]
                before = far[kv][lane * share + h, rows, :]
                merged[kv, h, rows, :] = jnp.where(inside, block, before)
            rise[kv][h].start()
            spread_across[kv][h].start()
            spread_pair[kv][h].start()
    up[1].start(level == 0)
    pass_on(1, level == 1)
    for kv in range(2):
        out_own[kv].arrived()
        out_far[kv].arrived()
        pass_low[kv].start()
        pass_high[kv].start()
    for kv in range(2):
        pair_own[kv].arrived()
        pair_far[kv].arrived()
        pass_low[kv].arrived()
        pass_high[kv].arrived()

    ns = slash.shape[1]
    groups = q_ref.shape[1] // (wk_ref.shape[0] * head_dim)
    back = lanes * blocks
    window_first = me * blocks - back
    scale = math.log2(math.e) / math.sqrt(head_dim)
    row = lax.broadcasted_iota(jnp.int32, (BS, head_dim), 0)
    col = lax.broadcasted_iota(jnp.int32, (BS, head_dim), 1)
    token = jnp.where(row == col, 1.0, 0.0).astype(kbuf.dtype)
    later = jnp.where((col < BS) & (row > col), MASKED, 0.0).astype(kbuf.dtype)
    vbuf[...] = jnp.ones_like(vbuf)

    def at_least_zero(number):
        return jnp.minimum(jnp.maximum(number + 1, 0), 1)

    def hide(active):
        shown = jnp.full((BS, head_dim), active, jnp.int32).astype(jnp.float32)
        return ((1.0 - shown) * MASKED).astype(kbuf.dtype)

    def rows_of(b):
        return slice(b * BS, (b + 1) * BS)

    def query_of(g, b):
        tiles = []
        for c in range(groups):
            first = pl.multiple_of((g * groups + c) * head_dim, head_dim)
            tiles.append(
                jnp.concatenate([q_ref[rows_of(b), pl.ds(first, head_dim)], token], axis=1)
            )
        return jnp.concatenate(tiles, axis=0)

    def score(g, b):
        return lax.dot_general(
            query_of(g, b), kbuf[b], (((1,), (1,)), ((), ())), preferred_element_type=jnp.float32
        )

    def attend_slash(g, carry):
        columns = pl.ds(pl.multiple_of(g * head_dim, head_dim), head_dim)
        offsets = [slash[g, m] for m in range(ns)]
        for b in range(blocks):
            for m in range(ns):
                rows = slice(m * BS, (m + 1) * BS)
                if m == 0:
                    at = back + b
                    kbuf[b, rows, head_dim:] = later
                else:
                    is_own = 1 - jnp.minimum(offsets[m], 1)
                    offset = offsets[m] + is_own * offsets[0]
                    active = at_least_zero(me * blocks + b - offset)
                    at = back + b - offset * active
                    kbuf[b, rows, head_dim:] = hide(active)
                kbuf[b, rows, :head_dim] = nk_ref[at, :, columns]
                vbuf[b, rows, :head_dim] = nv_ref[at, :, columns]
        for b in range(blocks):
            scores = score(g, b)
            row_max = jnp.max(scores, axis=-1, keepdims=True)
            weights = jnp.exp2((scores - row_max) * scale).astype(kbuf.dtype)
            both = jnp.dot(weights, vbuf[b], preferred_element_type=jnp.float32)
            mixed[g, b] = both[:, :head_dim]
            total[g, b] = both[:, head_dim:]
            top[g, b] = jnp.broadcast_to(row_max, top.shape[2:])
        return carry

    def attend_vertical(g, carry):
        columns = pl.ds(pl.multiple_of(g * head_dim, head_dim), head_dim)
        offsets = [slash[g, m] for m in range(ns)]
        for b in range(blocks):
            query_block = me * blocks + b
            for m in range(nv):
                rows = slice(m * BS, (m + 1) * BS)
                j = vertical[g, m]
                active = at_least_zero(query_block - j)
                for offset in offsets:
                    gap = query_block - j - offset
                    active = active * jnp.minimum(jnp.maximum(gap, -gap), 1)
                inside = at_least_zero(j - window_first)
                far_here = active * (1 - inside)
                at = back + b + active * inside * (j - window_first - back - b)
                use_far = jnp.full((BS, head_dim), far_here, jnp.int32) > 0
                kbuf[b, rows, head_dim:] = hide(active)
                kbuf[b, rows, :head_dim] = jnp.where(
                    use_far, wk_ref[g, rows, :], nk_ref[at, :, columns]
                )
                vbuf[b, rows, :head_dim] = jnp.where(
                    use_far, wv_ref[g, rows, :], nv_ref[at, :, columns]
                )
        for b in range(blocks):
            scores = score(g, b)
            old_max = top[g, b]
            row_max = jnp.maximum(old_max, jnp.max(scores, axis=-1, keepdims=True))
            keep = jnp.exp2((old_max - row_max) * scale)
            weights = jnp.exp2((scores - row_max[:, :1]) * scale).astype(kbuf.dtype)
            both = jnp.dot(weights, vbuf[b], preferred_element_type=jnp.float32)
            result = (mixed[g, b] * keep + both[:, :head_dim]) / (
                total[g, b] * keep + both[:, head_dim:]
            )
            result = result.astype(o_ref.dtype)
            for c in range(groups):
                first = pl.multiple_of((g * groups + c) * head_dim, head_dim)
                o_ref[rows_of(b), pl.ds(first, head_dim)] = result[rows_of(c)]
        return carry

    heads = wk_ref.shape[0]
    lax.fori_loop(0, heads, attend_slash, 0)
    for kv in range(2):
        for h in range(share):
            spread_across[kv][h].arrived()
            spread_last[kv][h].start()
    for kv in range(2):
        for h in range(share):
            spread_pair[kv][h].arrived()
            spread_last[kv][h].arrived()
    lax.fori_loop(0, heads, attend_vertical, 0)
    for each in links:
        each.sent()


def on_device(query_here, key_here, value_here, vertical_here, slash_here):
    tokens, width = key_here.shape
    kv_heads, nv = vertical_here.shape
    ns = slash_here.shape[1]
    head_dim = width // kv_heads
    groups = query_here.shape[1] // width
    lanes = -(-((SPAN - 1) * BS) // tokens)
    share = kv_heads // lanes
    blocks = tokens // BS
    kind = key_here.dtype
    anywhere = pl.BlockSpec(memory_space=pl.ANY)
    scalars = pl.BlockSpec(memory_space=pltpu.SMEM)
    near = pltpu.VMEM(((lanes + 1) * blocks, BS, width), kind)
    far = pltpu.VMEM((kv_heads, nv * BS, head_dim), kind)
    part = pltpu.VMEM((lanes * blocks, BS, share * head_dim), kind)
    slots = max(ns, nv) * BS
    operand = pltpu.VMEM((blocks, slots, 2 * head_dim), kind)
    state = pltpu.VMEM((kv_heads, blocks, groups * BS, head_dim), jnp.float32)
    copies = 2 * (lanes - 1 + 7 + 4 * share)
    return pl.pallas_call(
        functools.partial(fused_kernel, lanes),
        in_specs=[anywhere, anywhere, anywhere, scalars, scalars],
        out_specs=pl.BlockSpec(memory_space=pltpu.VMEM),
        out_shape=jax.ShapeDtypeStruct(query_here.shape, query_here.dtype),
        scratch_shapes=[
            pltpu.VMEM(query_here.shape, query_here.dtype),
            near,
            near,
            far,
            far,
            part,
            part,
            pltpu.VMEM((2, share, nv * BS, head_dim), kind),
            operand,
            operand,
            state,
            state,
            state,
            pltpu.SemaphoreType.DMA((copies,)),
            pltpu.SemaphoreType.DMA((copies,)),
            pltpu.SemaphoreType.DMA((5,)),
        ],
        compiler_params=pltpu.CompilerParams(
            collective_id=0, has_side_effects=True, vmem_limit_bytes=56 * 1024 * 1024
        ),
    )(
        query_here,
        key_here.reshape(blocks, BS, width),
        value_here.reshape(blocks, BS, width),
        vertical_here,
        slash_here,
    )


def solution(mesh):
    in_specs = (
        P(("parts", "seq", "head"), None),
        P(("parts", "seq", "head"), None),
        P(("parts", "seq", "head"), None),
        P("parts", None),
        P("parts", None),
    )
    out_specs = P(("parts", "seq", "head"), None)
    return jax.shard_map(
        on_device, mesh=mesh, in_specs=in_specs, out_specs=out_specs, check_vma=False
    )
```

time: 56 us -> 64.6 us (1.15); the launches traced: 55.1 us -> 64.4 us
  Pallas kernels: 49.5 us -> 61.3 us
  local copies, waits for them, and re-layouts: 5.54 us -> 3.1 us
    pallas_call x2 -> x1, Pallas kernels: 49.5 us -> 61.3 us  [on_device(): pl.pallas_call(functools.partial(fused_kernel, lanes), in_specs=[anywhere...]
    unnamed x12 -> x1, local copies, waits for them, and re-layouts: 5.54 us -> 3.1 us
where the time goes in v4:
time: 64.6 us; the launch traced here: 64.4 us
  Pallas kernels  61.3 us (95%)
  local copies, waits for them, and re-layouts  3.1 us (5%)
    pallas_call x1, Pallas kernels, on_device(): pl.pallas_call(functools.partial(fused_kernel, lanes), in_specs=[anywhere...  61.3 us
    unnamed x1, local copies, waits for them, and re-layouts  3.1 us

profile of v4, /device:TPU:8, one launch (start us, length us, event | category | flops | bytes accessed | tf_op | source)
XLA Modules:
  0.0 64.4 jit_solution(12507401765573720353)
XLA Ops:
  0.0 61.3 %shard_map.55 = bf16[128,8192]{1,0:T(8,128)(2,1)} custom-call(bf16[128,8192]{1,0:T(8,128)(2,1)} %q_hbm.1, bf16[2,64,1024]{2,1,0:T(8,128)(2,1)} %bitcast.2, bf16[2,64,1024]{2,1,0:T(8,128)(2,1)} %bitcast.3, s32[8,6]{1,0:T(8,128)} %vertical.1, s32[8,6]{1,0:T(8,128)} %slash.1), custom_call_target="tpu_custom_call" | custom-call | tf_op jit(solution)/shard_map/pallas_call | solution.py:361
  61.3 3.1 %copy.7 = bf16[128,8192]{1,0:T(8,128)(2,1)} copy(bf16[128,8192]{1,0:T(8,128)(2,1)} %shard_map.55) | data formatting | bytes 4194304

commit v5 on v3

--- a/solution.py
+++ b/solution.py
@@ -17,7 +17,20 @@
 
 
 def gather_kernel(
-    lanes, k_ref, v_ref, vertical, nk_ref, nv_ref, wk_ref, wv_ref, parts_k, parts_v, merged, send, recv
+    lanes,
+    k_ref,
+    v_ref,
+    vertical,
+    nk_ref,
+    nv_ref,
+    wk_ref,
+    wv_ref,
+    parts_k,
+    parts_v,
+    merged,
+    send,
+    recv,
+    local,
 ):
     cores = lax.axis_size("head")
     levels = lax.axis_size("seq") * cores // lanes
@@ -140,9 +153,16 @@
         out_own[kv].start()
         pair_own[kv].start()
     my_columns = pl.ds(pl.multiple_of(lane * width, width), width)
-    for kv in range(2):
-        parts[kv][mine] = own[kv][:, :, my_columns]
-        slot(near[kv], 0)[...] = own[kv][...]
+    kept = []
+    for kv in range(2):
+        kept.append((own[kv].at[:, :, my_columns], parts[kv].at[mine]))
+        kept.append((own[kv], slot(near[kv], 0)))
+    kept = [
+        pltpu.make_async_copy(source, target, local.at[i])
+        for i, (source, target) in enumerate(kept)
+    ]
+    for copy in kept:
+        copy.start()
 
     @pl.when(level == 0)
     def _():
@@ -158,6 +178,8 @@
 
     for part in split[: lanes - 1]:
         part.arrived()
+    for copy in kept:
+        copy.wait()
     pass_on(0)
     pass_on(1, level > 1)
     for kv in range(2):
@@ -210,13 +232,14 @@
     lanes = -(-((SPAN - 1) * BS) // tokens)
     share = kv_heads // lanes
     vmem = pl.BlockSpec(memory_space=pltpu.VMEM)
+    anywhere = pl.BlockSpec(memory_space=pl.ANY)
     blocks = tokens // BS
     near = jax.ShapeDtypeStruct(((lanes + 1) * blocks, BS, width), key_here.dtype)
     far = jax.ShapeDtypeStruct((kv_heads, nv * BS, head_dim), key_here.dtype)
     copies = 2 * (lanes - 1 + 7 + 4 * share)
     near_keys, near_values, far_keys, far_values = pl.pallas_call(
         functools.partial(gather_kernel, lanes),
-        in_specs=[vmem, vmem, pl.BlockSpec(memory_space=pltpu.SMEM)],
+        in_specs=[anywhere] * 2 + [pl.BlockSpec(memory_space=pltpu.SMEM)],
         out_specs=[vmem] * 4,
         out_shape=[near, near, far, far],
         scratch_shapes=[
@@ -225,12 +248,15 @@
             pltpu.VMEM((2, share, nv * BS, head_dim), key_here.dtype),
             pltpu.SemaphoreType.DMA((copies,)),
             pltpu.SemaphoreType.DMA((copies,)),
+            pltpu.SemaphoreType.DMA((4,)),
         ],
         compiler_params=pltpu.CompilerParams(
-            collective_id=0, has_side_effects=True, vmem_limit_bytes=16 * 1024 * 1024
+            collective_id=0, has_side_effects=True, vmem_limit_bytes=56 * 1024 * 1024
         ),
     )(
-        key_here.reshape(blocks, BS, width), value_here.reshape(blocks, BS, width), vertical_here
+        key_here.reshape(blocks, BS, width),
+        value_here.reshape(blocks, BS, width),
+        vertical_here,
     )
     return near_keys.reshape(-1, width), near_values.reshape(-1, width), far_keys, far_values
 
@@ -293,23 +319,35 @@
             if m > 0:
                 hidden = jnp.full((BS, head_dim), jnp.where(active, 0.0, MASKED), jnp.float32)
                 kbuf[b, rows, head_dim:] = hidden.astype(kbuf.dtype)
+
+    chunk = max(groups // 2, 1)
+
+    def score(b, first):
         q_rows = slice(b * BS, (b + 1) * BS)
         query = jnp.concatenate(
             [
                 jnp.concatenate([q_ref[q_rows, c * head_dim : (c + 1) * head_dim], token], axis=1)
-                for c in range(groups)
+                for c in range(first, first + chunk)
             ],
             axis=0,
         )
-        scores = lax.dot_general(
+        return lax.dot_general(
             query, kbuf[b], (((1,), (1,)), ((), ())), preferred_element_type=jnp.float32
         )
+
+    steps = [(b, first) for b in range(block_count) for first in range(0, groups, chunk)]
+    ahead = score(*steps[0])
+    for i, (b, first) in enumerate(steps):
+        scores = ahead
+        if i + 1 < len(steps):
+            ahead = score(*steps[i + 1])
         row_max = jnp.max(scores, axis=-1, keepdims=True)
         weights = jnp.exp2((scores - row_max) * scale).astype(jnp.bfloat16)
         mixed = jnp.dot(weights, vbuf[b], preferred_element_type=jnp.float32)
         mixed = (mixed[:, :head_dim] / mixed[:, head_dim:]).astype(o_ref.dtype)
-        for c in range(groups):
-            o_ref[q_rows, c * head_dim : (c + 1) * head_dim] = mixed[c * BS : (c + 1) * BS]
+        for c in range(chunk):
+            columns = slice((first + c) * head_dim, (first + c + 1) * head_dim)
+            o_ref[b * BS : (b + 1) * BS, columns] = mixed[c * BS : (c + 1) * BS]
 
 
 def attend(query_here, near_keys, near_values, far_keys, far_values, vertical_here, slash_here):
@@ -337,7 +375,7 @@
         ),
         out_shape=jax.ShapeDtypeStruct((length, width), query_here.dtype),
         compiler_params=pltpu.CompilerParams(
-            dimension_semantics=("arbitrary",), vmem_limit_bytes=24 * 1024 * 1024
+            dimension_semantics=("arbitrary",), vmem_limit_bytes=58 * 1024 * 1024
         ),
         cost_estimate=pl.CostEstimate(
             flops=4 * length * width * slots,

time: 56 us -> 51 us (0.911)
  local copies, waits for them, and re-layouts: 5.54 us -> 0 us
  Pallas kernels: 49.5 us -> 50.2 us
    unnamed x12 -> x0, local copies, waits for them, and re-layouts: 5.54 us -> none
    pallas_call x1, Pallas kernels: 33.1 us -> 35.5 us  [gather(): pl.pallas_call(functools.partial(gather_kernel, lanes), in_specs=[anywher...]
    pallas_call x1, Pallas kernels: 16.4 us -> 14.7 us  [attend(): pl.pallas_call(attention_kernel, grid_spec=pltpu.PrefetchScalarGridSpec(n...]
where the time goes in v5:
time: 51 us; the launch traced here: 50.2 us
  Pallas kernels  50.2 us (98%)
    pallas_call x1, Pallas kernels, gather(): pl.pallas_call(functools.partial(gather_kernel, lanes), in_specs=[anywher...  35.5 us
    pallas_call x1, Pallas kernels, attend(): pl.pallas_call(attention_kernel, grid_spec=pltpu.PrefetchScalarGridSpec(n...  14.7 us

profile of v5, /device:TPU:8, one launch (start us, length us, event | category | flops | bytes accessed | tf_op | source)
XLA Modules:
  0.0 50.2 jit_solution(16555997555257368182)
XLA Ops:
  0.0 35.5 %shard_map.55 = (bf16[10,64,1024]{2,1,0:T(8,128)(2,1)}, bf16[10,64,1024]{2,1,0:T(8,128)(2,1)}, bf16[8,384,128]{2,1,0:T(8,128)(2,1)}, bf16[8,384,128]{2,1,0:T(8,128)(2,1)}) custom-call(bf16[2,64,1024]{2,1,0:T(8,128)(2,1)} %bitcast.4, bf16[2,64,1024]{2,1,0:T(8,128)(2,1)} %bitcast.5, s32[8,6]{1,0:T(8,128)} %vertical.3), custom_call_target="tpu_custom_call" | custom-call | tf_op jit(solution)/shard_map/pallas_call | solution.py:240
  35.5 14.7 %shard_map.56 = bf16[128,8192]{1,0:T(8,128)(2,1)} custom-call(s32[8,6]{1,0:T(8,128)} %vertical.3, s32[8,6]{1,0:T(8,128)} %slash.1, bf16[128,8192]{1,0:T(8,128)(2,1)} %q_ref.1, bf16[640,1024]{1,0:T(8,128)(2,1)} %bitcast.6, bf16[640,1024]{1,0:T(8,128)(2,1)} %bitcast.7, bf16[8,384,128]{2,1,0:T(8,128)(2,1)} %get-tuple-element.11.wk_ref, ...), custom_call_target="tpu_custom_call" | custom-call | flops 3221225472 | bytes 4194304 | tf_op jit(solution)/shard_map/pallas_call | solution.py:364

commit v6 on v5

--- a/solution.py
+++ b/solution.py
@@ -264,11 +264,11 @@
 def attention_kernel(
     vertical, slash, q_ref, nk_ref, nv_ref, wk_ref, wv_ref, o_ref, kbuf, vbuf
 ):
-    g = pl.program_id(0)
+    step = pl.program_id(0)
     position = lax.axis_index(("seq", "head"))
     tokens = q_ref.shape[0]
-    head_dim = nk_ref.shape[1]
-    groups = q_ref.shape[1] // head_dim
+    heads, head_dim = wk_ref.shape[0], wk_ref.shape[2]
+    groups = q_ref.shape[1] // (heads * head_dim)
     block_count = tokens // BS
     window_blocks = nk_ref.shape[0] // BS
     back_blocks = window_blocks - block_count
@@ -280,19 +280,21 @@
     col = lax.broadcasted_iota(jnp.int32, (BS, head_dim), 1)
     token = jnp.where(row == col, 1.0, 0.0).astype(kbuf.dtype)
 
-    @pl.when(g == 0)
+    @pl.when(step == 0)
     def _():
         vbuf[...] = jnp.ones_like(vbuf)
         later = jnp.where((col < BS) & (row > col), MASKED, 0.0).astype(kbuf.dtype)
-        for b in range(block_count):
-            kbuf[b, :BS, head_dim:] = later
-
-    offsets = [slash[g, m] for m in range(ns)]
-    columns = [vertical[g, m] for m in range(nv)]
-    ordered = [jnp.int32(0)] + [
-        jnp.where(offsets[m] == 0, offsets[0], offsets[m]) for m in range(1, ns)
-    ]
-    for b in range(block_count):
+        for n in range(heads * block_count):
+            kbuf[n, :BS, head_dim:] = later
+
+    def fill(head, b):
+        g = step * heads + head
+        n = head * block_count + b
+        offsets = [slash[g, m] for m in range(ns)]
+        ordered = [jnp.int32(0)] + [
+            jnp.where(offsets[m] == 0, offsets[0], offsets[m]) for m in range(1, ns)
+        ]
+        lanes = slice(head * head_dim, (head + 1) * head_dim)
         query_block = position * block_count + b
         own = back_blocks + b
         for m in range(ns + nv):
@@ -301,10 +303,10 @@
                 active = ordered[m] <= query_block
                 at = jnp.where(active, own - ordered[m], own)
                 at = pl.multiple_of(at * BS, BS)
-                key_block = nk_ref[pl.ds(at, BS), :]
-                value_block = nv_ref[pl.ds(at, BS), :]
+                key_block = nk_ref[pl.ds(at, BS), lanes]
+                value_block = nv_ref[pl.ds(at, BS), lanes]
             else:
-                j = columns[m - ns]
+                j = vertical[g, m - ns]
                 active = j <= query_block
                 for off in offsets:
                     active = active & (query_block - j != off)
@@ -312,42 +314,61 @@
                 at = jnp.where(active & near, j - window_first, own)
                 at = pl.multiple_of(at * BS, BS)
                 far_rows = pl.ds((m - ns) * BS, BS)
-                key_block = jnp.where(near, nk_ref[pl.ds(at, BS), :], wk_ref[0, far_rows, :])
-                value_block = jnp.where(near, nv_ref[pl.ds(at, BS), :], wv_ref[0, far_rows, :])
-            kbuf[b, rows, :head_dim] = key_block
-            vbuf[b, rows, :head_dim] = value_block
+                key_block = jnp.where(near, nk_ref[pl.ds(at, BS), lanes], wk_ref[head, far_rows, :])
+                value_block = jnp.where(
+                    near, nv_ref[pl.ds(at, BS), lanes], wv_ref[head, far_rows, :]
+                )
+            kbuf[n, rows, :head_dim] = key_block
+            vbuf[n, rows, :head_dim] = value_block
             if m > 0:
                 hidden = jnp.full((BS, head_dim), jnp.where(active, 0.0, MASKED), jnp.float32)
-                kbuf[b, rows, head_dim:] = hidden.astype(kbuf.dtype)
+                kbuf[n, rows, head_dim:] = hidden.astype(kbuf.dtype)
 
     chunk = max(groups // 2, 1)
 
-    def score(b, first):
+    def columns_of(head, c):
+        first = (head * groups + c) * head_dim
+        return slice(first, first + head_dim)
+
+    def score(head, b, first):
+        if first == 0:
+            fill(head, b)
         q_rows = slice(b * BS, (b + 1) * BS)
         query = jnp.concatenate(
             [
-                jnp.concatenate([q_ref[q_rows, c * head_dim : (c + 1) * head_dim], token], axis=1)
+                jnp.concatenate([q_ref[q_rows, columns_of(head, c)], token], axis=1)
                 for c in range(first, first + chunk)
             ],
             axis=0,
         )
         return lax.dot_general(
-            query, kbuf[b], (((1,), (1,)), ((), ())), preferred_element_type=jnp.float32
+            query,
+            kbuf[head * block_count + b],
+            (((1,), (1,)), ((), ())),
+            preferred_element_type=jnp.float32,
         )
 
-    steps = [(b, first) for b in range(block_count) for first in range(0, groups, chunk)]
+    steps = [
+        (head, b, first)
+        for head in range(heads)
+        for b in range(block_count)
+        for first in range(0, groups, chunk)
+    ]
     ahead = score(*steps[0])
-    for i, (b, first) in enumerate(steps):
+    for i, (head, b, first) in enumerate(steps):
         scores = ahead
         if i + 1 < len(steps):
             ahead = score(*steps[i + 1])
         row_max = jnp.max(scores, axis=-1, keepdims=True)
         weights = jnp.exp2((scores - row_max) * scale).astype(jnp.bfloat16)
-        mixed = jnp.dot(weights, vbuf[b], preferred_element_type=jnp.float32)
+        mixed = jnp.dot(
+            weights, vbuf[head * block_count + b], preferred_element_type=jnp.float32
+        )
         mixed = (mixed[:, :head_dim] / mixed[:, head_dim:]).astype(o_ref.dtype)
         for c in range(chunk):
-            columns = slice((first + c) * head_dim, (first + c + 1) * head_dim)
-            o_ref[b * BS : (b + 1) * BS, columns] = mixed[c * BS : (c + 1) * BS]
+            o_ref[b * BS : (b + 1) * BS, columns_of(head, first + c)] = mixed[
+                c * BS : (c + 1) * BS
+            ]
 
 
 def attend(query_here, near_keys, near_values, far_keys, far_values, vertical_here, slash_here):
@@ -357,20 +378,21 @@
     head_dim = near_keys.shape[1] // kv_heads
     group_width = width // kv_heads
     block_count = length // BS
-    near_spec = pl.BlockSpec((near_keys.shape[0], head_dim), lambda g, *_: (0, g))
-    far_spec = pl.BlockSpec((1, nv * BS, head_dim), lambda g, *_: (g, 0, 0))
-    row_spec = pl.BlockSpec((length, group_width), lambda g, *_: (0, g))
+    heads = 2 if kv_heads % 2 == 0 else 1
+    near_spec = pl.BlockSpec((near_keys.shape[0], heads * head_dim), lambda g, *_: (0, g))
+    far_spec = pl.BlockSpec((heads, nv * BS, head_dim), lambda g, *_: (g, 0, 0))
+    row_spec = pl.BlockSpec((length, heads * group_width), lambda g, *_: (0, g))
     slots = (ns + nv) * BS
     return pl.pallas_call(
         attention_kernel,
         grid_spec=pltpu.PrefetchScalarGridSpec(
             num_scalar_prefetch=2,
-            grid=(kv_heads,),
+            grid=(kv_heads // heads,),
             in_specs=[row_spec, near_spec, near_spec, far_spec, far_spec],
             out_specs=row_spec,
             scratch_shapes=[
-                pltpu.VMEM((block_count, slots, 2 * head_dim), jnp.bfloat16),
-                pltpu.VMEM((block_count, slots, 2 * head_dim), jnp.bfloat16),
+                pltpu.VMEM((heads * block_count, slots, 2 * head_dim), jnp.bfloat16),
+                pltpu.VMEM((heads * block_count, slots, 2 * head_dim), jnp.bfloat16),
             ],
         ),
         out_shape=jax.ShapeDtypeStruct((length, width), query_here.dtype),

time: 51 us -> 49.7 us (0.975)
  Pallas kernels: 50.2 us -> 48.9 us
    pallas_call x1, Pallas kernels: 14.7 us -> 13.4 us  [attend(): pl.pallas_call(attention_kernel, grid_spec=pltpu.PrefetchScalarGridSpec(n...]
where the time goes in v6:
time: 49.7 us; the launch traced here: 48.9 us
  Pallas kernels  48.9 us (98%)
    pallas_call x1, Pallas kernels, gather(): pl.pallas_call(functools.partial(gather_kernel, lanes), in_specs=[anywher...  35.5 us
    pallas_call x1, Pallas kernels, attend(): pl.pallas_call(attention_kernel, grid_spec=pltpu.PrefetchScalarGridSpec(n...  13.4 us

profile of v6, /device:TPU:8, one launch (start us, length us, event | category | flops | bytes accessed | tf_op | source)
XLA Modules:
  0.0 48.9 jit_solution(2494663558916897947)
XLA Ops:
  0.0 35.5 %shard_map.55 = (bf16[10,64,1024]{2,1,0:T(8,128)(2,1)}, bf16[10,64,1024]{2,1,0:T(8,128)(2,1)}, bf16[8,384,128]{2,1,0:T(8,128)(2,1)}, bf16[8,384,128]{2,1,0:T(8,128)(2,1)}) custom-call(bf16[2,64,1024]{2,1,0:T(8,128)(2,1)} %bitcast.4, bf16[2,64,1024]{2,1,0:T(8,128)(2,1)} %bitcast.5, s32[8,6]{1,0:T(8,128)} %vertical.3), custom_call_target="tpu_custom_call" | custom-call | tf_op jit(solution)/shard_map/pallas_call | solution.py:240
  35.5 13.4 %shard_map.56 = bf16[128,8192]{1,0:T(8,128)(2,1)} custom-call(s32[8,6]{1,0:T(8,128)} %vertical.3, s32[8,6]{1,0:T(8,128)} %slash.1, bf16[128,8192]{1,0:T(8,128)(2,1)} %q_ref.1, bf16[640,1024]{1,0:T(8,128)(2,1)} %bitcast.6, bf16[640,1024]{1,0:T(8,128)(2,1)} %bitcast.7, bf16[8,384,128]{2,1,0:T(8,128)(2,1)} %get-tuple-element.11.wk_ref, ...), custom_call_target="tpu_custom_call" | custom-call | flops 3221225472 | bytes 4194304 | tf_op jit(solution)/shard_map/pallas_call | solution.py:386

commit v7 on v6

--- a/solution.py
+++ b/solution.py
@@ -364,7 +364,10 @@
         mixed = jnp.dot(
             weights, vbuf[head * block_count + b], preferred_element_type=jnp.float32
         )
-        mixed = (mixed[:, :head_dim] / mixed[:, head_dim:]).astype(o_ref.dtype)
+        row_total = mixed[:, head_dim:]
+        inverse = pl.reciprocal(row_total, approx=True)
+        inverse = inverse * (2.0 - row_total * inverse)
+        mixed = (mixed[:, :head_dim] * inverse).astype(o_ref.dtype)
         for c in range(chunk):
             o_ref[b * BS : (b + 1) * BS, columns_of(head, first + c)] = mixed[
                 c * BS : (c + 1) * BS

time: 49.7 us -> 50 us (level)
  no operation moved by 1% of the time
where the time goes in v7:
time: 50 us; the launch traced here: 49.2 us
  Pallas kernels  49.2 us (98%)
    pallas_call x1, Pallas kernels, gather(): pl.pallas_call(functools.partial(gather_kernel, lanes), in_specs=[anywher...  35.5 us
    pallas_call x1, Pallas kernels, attend(): pl.pallas_call(attention_kernel, grid_spec=pltpu.PrefetchScalarGridSpec(n...  13.7 us

profile of v7, /device:TPU:8, one launch (start us, length us, event | category | flops | bytes accessed | tf_op | source)
XLA Modules:
  0.0 49.2 jit_solution(8603957669685491418)
XLA Ops:
  0.0 35.5 %shard_map.55 = (bf16[10,64,1024]{2,1,0:T(8,128)(2,1)}, bf16[10,64,1024]{2,1,0:T(8,128)(2,1)}, bf16[8,384,128]{2,1,0:T(8,128)(2,1)}, bf16[8,384,128]{2,1,0:T(8,128)(2,1)}) custom-call(bf16[2,64,1024]{2,1,0:T(8,128)(2,1)} %bitcast.4, bf16[2,64,1024]{2,1,0:T(8,128)(2,1)} %bitcast.5, s32[8,6]{1,0:T(8,128)} %vertical.3), custom_call_target="tpu_custom_call" | custom-call | tf_op jit(solution)/shard_map/pallas_call | solution.py:240
  35.5 13.7 %shard_map.56 = bf16[128,8192]{1,0:T(8,128)(2,1)} custom-call(s32[8,6]{1,0:T(8,128)} %vertical.3, s32[8,6]{1,0:T(8,128)} %slash.1, bf16[128,8192]{1,0:T(8,128)(2,1)} %q_ref.1, bf16[640,1024]{1,0:T(8,128)(2,1)} %bitcast.6, bf16[640,1024]{1,0:T(8,128)(2,1)} %bitcast.7, bf16[8,384,128]{2,1,0:T(8,128)(2,1)} %get-tuple-element.11.wk_ref, ...), custom_call_target="tpu_custom_call" | custom-call | flops 3221225472 | bytes 4194304 | tf_op jit(solution)/shard_map/pallas_call | solution.py:389
